TPU v7x, 256 devices: a whole 4x4x8 slice. The times are simulated.
256 devices in a mesh: gx: 16 (over y, z_hi), gy: 4 (over z_lo, core), gz: 4 (over x).
Axes of the slice: x: 4, y: 4, z: 8 (z_hi: 4, z_lo: 2; z = z_hi * 2 + z_lo), core: 2. Of those that a mesh axis runs over, the one named last changes fastest.
Arguments:
- permeability: float32 [3, 128, 32, 512], P(None, 'gx', 'gy', 'gz'), may hold values from 0.001 to 0.1
- well_flags: int32 [128, 32, 512], P('gx', 'gy', 'gz'), may hold values 0 or 1
- support_mask: int32 [8, 128, 32, 512], P(None, 'gx', 'gy', 'gz'), may hold values from 0 to 1, as said below
Outputs:
- prolongation: float32 [8, 128, 32, 512], P(None, 'gx', 'gy', 'gz')
- coarse_matrix: float32 [3, 3, 3, 16, 4, 64], P(None, None, None, 'gx', 'gy', 'gz')
Inputs may be any that keep to these rules, and one draw needn't show every extreme that they name: support_mask[s] at a cell is 1 exactly where the cell lies in the support of the coarse block named by slot s at that cell; each block's support is a box that holds the block itself and reaches between 0 and half a block's edge into the neighbouring blocks on each side along each dimension, and is 0 for blocks outside the grid; so a cell's own-block slot is always 1.
All inputs are finite; a program needn't handle non-finite values. No bound on the sum of `well_flags` on one device may be relied on, other than what follows from the above.
Results may differ from a plain program's by a relative error of at most 0.0003.
Values sent between devices are 32-bit elements; how exact they have to be, the bound alone decides.
A program may use at most 128 MiB of HBM per device.

v0:
```python
import jax
import jax.numpy as jnp
from jax import lax
from jax.experimental import pallas as pl
from jax.experimental.pallas import tpu as pltpu
from jax.sharding import PartitionSpec as P

MESH = pl.DeviceIdType.MESH
AXES = ("gx", "gy", "gz")
COUNT = {"gx": 16, "gy": 4, "gz": 4}
SWEEPS = 4
STEP = 2.0 / 3.0
WELL = 0.05
E = 8
LANES = 128
ROW0 = 8


def harmonic(lower, upper):
    return 2.0 * lower * upper / (lower + upper)


def kernel(
    perm, flags, mask, out_p, out_c,
    kx, ky, kz, kz_send, kz_halo, fl, mk, basis, z_send, z_halo,
    vx, vy, vz, negdiag, part, pz, iz, sums, rows, rows_x, rows_y, rows_d, zr_send, zr_halo,
    load_sem, k_send, k_recv, p_send, p_recv, zr_ssem, zr_rsem, r_send, r_recv, out_sem,
):
    at = {axis: lax.axis_index(axis) for axis in AXES}
    has = {}
    for axis in AXES:
        has[axis, 1] = at[axis] < COUNT[axis] - 1
        has[axis, -1] = at[axis] > 0
    par_x, par_y = lax.rem(at["gx"], 2), lax.rem(at["gy"], 2)
    lane = lax.broadcasted_iota(jnp.int32, (E, LANES), 1)
    row = lax.broadcasted_iota(jnp.int32, (E, LANES), 0)
    even = lax.rem(lane // E, 2) == 0

    loads = [
        pltpu.make_async_copy(perm.at[0], kx.at[pl.ds(1, E)], load_sem.at[0]),
        pltpu.make_async_copy(perm.at[1], ky.at[:, pl.ds(ROW0, E)], load_sem.at[1]),
        pltpu.make_async_copy(perm.at[2], kz, load_sem.at[2]),
        pltpu.make_async_copy(flags, fl, load_sem.at[3]),
        pltpu.make_async_copy(mask, mk, load_sem.at[4]),
    ]
    for load in loads:
        load.start()

    barrier = pltpu.get_barrier_semaphore()
    expected = 0
    for axis in AXES:
        for d in (1, -1):
            @pl.when(has[axis, d])
            def _():
                pl.semaphore_signal(
                    barrier, inc=1, device_id={axis: at[axis] + d}, device_id_type=MESH
                )
            expected = expected + has[axis, d].astype(jnp.int32)

    def shift_to(axis, d):
        size = COUNT[axis]
        return lax.rem(at[axis] + d + size, size)

    class Copy:
        def __init__(self, src, dst, ssem, rsem, moves):
            self.send_if = None
            self.recv_if = None
            target = {}
            for axis, d in moves:
                target[axis] = shift_to(axis, d)
                s, r = has[axis, d], has[axis, -d]
                self.send_if = s if self.send_if is None else self.send_if & s
                self.recv_if = r if self.recv_if is None else self.recv_if & r
            self.copy = pltpu.make_async_remote_copy(
                src_ref=src, dst_ref=dst, send_sem=ssem, recv_sem=rsem,
                device_id=target, device_id_type=MESH,
            )

        def start(self):
            pl.when(self.send_if)(self.copy.start)

        def wait_recv(self):
            pl.when(self.recv_if)(self.copy.wait_recv)

        def wait_send(self):
            pl.when(self.send_if)(self.copy.wait_send)

    started = []

    def start(copies):
        for c in copies:
            c.start()
        started.extend(copies)

    def fill(i, carry):
        s, x = i // 10, lax.rem(i, 10)
        bx, by, bz = s // 4, lax.rem(s // 2, 2), lax.rem(s, 2)
        block_x = jnp.where((x == 0) | (x == 9), 1 - par_x, par_x)
        hot_x = (bx == block_x).astype(jnp.float32)
        own_y = (by == par_y).astype(jnp.float32)
        hot_z = jnp.where(lax.rem(lane // E, 2) == bz, hot_x, 0.0)
        basis[0, s, x, 0:8] = hot_z * (1.0 - own_y)
        basis[0, s, x, 8:16] = hot_z * own_y
        basis[0, s, x, 16:24] = hot_z * (1.0 - own_y)
        return carry

    lax.fori_loop(0, 80, fill, 0)
    slot = lane // E
    hot_xy = (slot // 4 == par_x) & (lax.rem(slot // 2, 2) == par_y)
    for side in range(2):
        z_halo[0, side] = jnp.where(hot_xy & (lax.rem(slot, 2) == 1 - side), 1.0, 0.0)

    zero = jnp.zeros((E, LANES), jnp.float32)
    for d, k_plane in ((-1, 0), (1, 9)):
        side = (d + 1) // 2

        @pl.when(jnp.logical_not(has["gx", d]))
        def _():
            kx[k_plane] = zero
            for k in range(1, SWEEPS + 1):
                basis[k, :, k_plane, 8:16] = jnp.zeros((8, E, LANES), jnp.float32)
            rows_x[side] = jnp.zeros((2, E, LANES), jnp.float32)

        @pl.when(jnp.logical_not(has["gy", d]))
        def _():
            y_row = 7 if d < 0 else 16
            ky[:, y_row:y_row + 1] = jnp.zeros((E, 1, LANES), jnp.float32)

            def clear(i, carry):
                basis[1 + i // 8, lax.rem(i, 8), 1:9, y_row:y_row + 1] = jnp.zeros(
                    (E, 1, LANES), jnp.float32
                )
                return carry

            lax.fori_loop(0, 8 * SWEEPS, clear, 0)
            rows_y[side] = jnp.zeros((2, E, LANES), jnp.float32)

        @pl.when(jnp.logical_not(has["gz", d]))
        def _():
            kz_halo[side] = zero
            for k in range(1, SWEEPS + 1):
                z_halo[k, side] = zero
            zr_halo[side] = zero

        for e in (1, -1):
            @pl.when(jnp.logical_not(has["gx", d] & has["gy", e]))
            def _():
                rows_d[side, (e + 1) // 2] = zero

    for load in loads[:3]:
        load.wait()
    for side in range(2):
        tile = zero
        for x in range(E):
            shift = (x - 127) % LANES if side == 0 else x
            moved = pltpu.roll(kz[x], shift, 1) if shift else kz[x]
            tile = jnp.where(lane == x, moved, tile)
        kz_send[side] = tile
    pl.semaphore_wait(barrier, expected)
    k_x = [
        Copy(kx.at[8], kx.at[0], k_send.at[0], k_recv.at[0], (("gx", 1),)),
        Copy(kx.at[1], kx.at[9], k_send.at[1], k_recv.at[1], (("gx", -1),)),
    ]
    k_yz = [
        Copy(ky.at[:, pl.ds(15, 1)], ky.at[:, pl.ds(7, 1)], k_send.at[2], k_recv.at[2], (("gy", 1),)),
        Copy(ky.at[:, pl.ds(8, 1)], ky.at[:, pl.ds(16, 1)], k_send.at[3], k_recv.at[3], (("gy", -1),)),
        Copy(kz_send.at[0], kz_halo.at[0], k_send.at[4], k_recv.at[4], (("gz", 1),)),
        Copy(kz_send.at[1], kz_halo.at[1], k_send.at[5], k_recv.at[5], (("gz", -1),)),
    ]
    start(k_x)
    start(k_yz)

    def weights(x):
        here = kx[x + 1]
        t_x = (harmonic(kx[x], here), harmonic(here, kx[x + 2]))
        here = ky[x, 8:16]
        t_y = (harmonic(ky[x, 7:15], here), harmonic(here, ky[x, 9:17]))
        here = kz[x]
        before = jnp.where(
            lane == 0, pltpu.roll(kz_halo[0], LANES - x, 1), pltpu.roll(here, 1, 1)
        )
        after = jnp.where(
            lane == 127, pltpu.roll(kz_halo[1], 127 - x, 1), pltpu.roll(here, 127, 1)
        )
        t_z = (harmonic(before, here), harmonic(here, after))
        diagonal = t_x[0] + t_x[1] + t_y[0] + t_y[1] + t_z[0] + t_z[1]
        diagonal = diagonal + WELL * fl[x].astype(jnp.float32)
        negdiag[x] = -1.5 * diagonal
        scale = STEP / diagonal
        for b in range(2):
            keep_x = (par_x == b).astype(jnp.float32)
            keep_y = (par_y == b).astype(jnp.float32)
            own_z = even if b == 0 else jnp.logical_not(even)
            for side in range(2):
                inner = 4 - side
                vx[b, side, x] = t_x[side] * scale * jnp.where(x == inner, keep_x, 1.0)
                vy[b, side, x] = t_y[side] * scale * jnp.where(row == inner, keep_y, 1.0)
                cut = (lax.rem(lane, E) == inner) & jnp.logical_not(own_z)
                vz[b, side, x] = jnp.where(cut, 0.0, t_z[side] * scale)

    def center_of(k, x):
        return basis[k, :, x + 1, 8:16].reshape(2, 2, 2, E, LANES)

    def flow_x(k, x, side):
        near = basis[k, :, x + 2 * side, 8:16].reshape(2, 2, 2, E, LANES)
        return vx[:, side, x][:, None, None] * near

    def flow_yz(k, x):
        center = basis[k, :, x + 1, 8:16]
        total = -STEP * center.reshape(2, 2, 2, E, LANES)
        for side in range(2):
            near = basis[k, :, x + 1, 7 + 2 * side:15 + 2 * side].reshape(2, 2, 2, E, LANES)
            total = total + vy[:, side, x][None, :, None] * near
            edge = lane == (0, 127)[side]
            halo = z_halo[k, side]
            moved = []
            for s in range(8):
                place = s * 8 + x
                shift = LANES - place if side == 0 else 127 - place
                moved.append(
                    jnp.where(
                        edge,
                        pltpu.roll(halo, shift, 1),
                        pltpu.roll(center[s], (1, 127)[side], 1),
                    )
                )
            near = jnp.stack(moved).reshape(2, 2, 2, E, LANES)
            total = total + vz[:, side, x][None, None] * near
        return total

    def update(k, x, flow):
        center = center_of(k, x)
        support = mk[:, x].astype(jnp.float32).reshape(2, 2, 2, E, LANES)
        change = support * flow
        change_sum = jnp.sum(change, axis=(0, 1, 2))
        fresh = center + change - center * change_sum
        basis[k + 1, :, x + 1, 8:16] = fresh.reshape(8, E, LANES)

    def pack_z(k, x, tiles):
        up, down = tiles
        for s in range(8):
            place = s * 8 + x
            value = basis[k, s, x + 1, 8:16]
            up = jnp.where(lane == place, pltpu.roll(value, place + 1, 1), up)
            down = jnp.where(lane == place, pltpu.roll(value, place, 1), down)
        return up, down

    def copies(k):
        ref = basis.at[k]
        own = pl.ds(8, E)
        planes = pl.ds(1, E)
        sems = [(p_send.at[k, i], p_recv.at[k, i]) for i in range(6)]
        x = [
            Copy(ref.at[:, 8, own], ref.at[:, 0, own], *sems[0], (("gx", 1),)),
            Copy(ref.at[:, 1, own], ref.at[:, 9, own], *sems[1], (("gx", -1),)),
        ]
        yz = [
            Copy(ref.at[:, planes, pl.ds(15, 1)], ref.at[:, planes, pl.ds(7, 1)], *sems[2], (("gy", 1),)),
            Copy(ref.at[:, planes, pl.ds(8, 1)], ref.at[:, planes, pl.ds(16, 1)], *sems[3], (("gy", -1),)),
            Copy(z_send.at[k, 0], z_halo.at[k, 0], *sems[4], (("gz", 1),)),
            Copy(z_send.at[k, 1], z_halo.at[k, 1], *sems[5], (("gz", -1),)),
        ]
        return x, yz

    def inner_flow(k, x):
        return flow_yz(k, x) + flow_x(k, x, 0) + flow_x(k, x, 1)

    arriving_x, arriving_yz = k_x, k_yz
    for k in range(SWEEPS):
        for c in arriving_yz:
            c.wait_recv()
        if k == 0:
            for load in loads[3:]:
                load.wait()

            def prepare(x, carry):
                weights(x)
                return carry

            lax.fori_loop(1, 7, prepare, 0)

        def inner(x, tiles):
            update(k, x, inner_flow(k, x))
            return pack_z(k + 1, x, tiles)

        tiles = lax.fori_loop(1, 7, inner, (zero, zero))
        if k > 0:
            for x, side in ((0, 1), (7, 0)):
                part[1 - side] = (flow_yz(k, x) + flow_x(k, x, side)).reshape(8, E, LANES)
        for c in arriving_x:
            c.wait_recv()
        arriving_x, arriving_yz = copies(k + 1)
        for x, side in ((0, 0), (7, 1)):
            if k == 0:
                weights(x)
                flow = inner_flow(k, x)
            else:
                flow = part[side].reshape(2, 2, 2, E, LANES) + flow_x(k, x, side)
            update(k, x, flow)
        start(arriving_x)
        for x in (0, 7):
            tiles = pack_z(k + 1, x, tiles)
        z_send[k + 1, 0], z_send[k + 1, 1] = tiles
        start(arriving_yz)

    out = pltpu.make_async_copy(
        basis.at[SWEEPS, :, pl.ds(1, E), pl.ds(8, E)], out_p, out_sem.at[0]
    )
    out.start()

    def split_z(values):
        pair = values.reshape(4, 2, E, LANES)
        return (
            jnp.where(even, pair[:, 0], pair[:, 1]),
            jnp.where(even, pair[:, 1], pair[:, 0]),
        )

    def image(x, flow):
        own, beside = split_z(flow * negdiag[x])
        iz[:, 0, x] = own
        iz[:, 1, x] = beside

    def split_basis(x, carry):
        own, beside = split_z(center_of(SWEEPS, x))
        pz[:, 0, x] = own
        pz[:, 1, x] = beside
        return carry

    lax.fori_loop(0, E, split_basis, 0)
    for c in arriving_yz:
        c.wait_recv()

    def inner_image(x, carry):
        image(x, inner_flow(SWEEPS, x))
        return carry

    lax.fori_loop(1, 7, inner_image, 0)
    for x, side in ((0, 1), (7, 0)):
        part[1 - side] = (flow_yz(SWEEPS, x) + flow_x(SWEEPS, x, side)).reshape(8, E, LANES)

    def contract(first):
        def body(i, carry):
            half, a_x, a_y = i // 4, lax.rem(i // 2, 2), lax.rem(i, 2)
            s_xy = lax.rem(a_x + par_x, 2) * 2 + lax.rem(a_y + par_y, 2)
            planes = [1 + 3 * half + j for j in range(3)] if first else [7 * half]
            for a_z in range(2):
                for e_x in range(2):
                    for e_y in range(2):
                        u_xy = lax.rem(a_x + e_x + par_x, 2) * 2 + lax.rem(a_y + e_y + par_y, 2)
                        for e_z in range(2):
                            e = e_x * 4 + e_y * 2 + e_z
                            base = pl.multiple_of((i * 2 + a_z) * 64, 64) + e * 8
                            total = None if first else sums[pl.ds(base, E)]
                            for x in planes:
                                term = pz[s_xy, a_z, x] * iz[u_xy, (a_z + e_z) % 2, x]
                                total = term if total is None else total + term
                            sums[pl.ds(base, E)] = total
            return carry

        lax.fori_loop(0, 8, body, 0)

    contract(True)
    for c in arriving_x:
        c.wait_recv()
    for x, side in ((0, 0), (7, 1)):
        image(x, part[side].reshape(2, 2, 2, E, LANES) + flow_x(SWEEPS, x, side))
    contract(False)

    quarter = []
    for y_half in range(2):
        total = sums[pl.ds(4 * y_half, LANES, stride=8)]
        for y in range(1, 4):
            total = total + sums[pl.ds(4 * y_half + y, LANES, stride=8)]
        total = total.reshape(16, E, LANES)
        total = total + pltpu.roll(total, 127, 2)
        total = total + pltpu.roll(total, 126, 2)
        quarter.append(total.reshape(8, 2, E, LANES))
    up, down = zero, zero
    for i in range(8):
        for y_half in range(2):
            place = i * 2 + y_half
            beside = quarter[y_half][i, 1]
            up = jnp.where(lane == place, pltpu.roll(beside, place + 4, 1), up)
            moved = pltpu.roll(beside, place, 1) if place else beside
            down = jnp.where(lane == place, moved, down)
    zr_send[0], zr_send[1] = up, down
    zr = [
        Copy(zr_send.at[0], zr_halo.at[0], zr_ssem.at[0], zr_rsem.at[0], (("gz", 1),)),
        Copy(zr_send.at[1], zr_halo.at[1], zr_ssem.at[1], zr_rsem.at[1], (("gz", -1),)),
    ]
    start(zr)
    low = (lax.rem(lane, E) == 0) & (lane != 0)
    high = (lax.rem(lane, E) == 4) & (lane != 124)
    merged = []
    for y_half in range(2):
        own, beside = quarter[y_half][:, 0], quarter[y_half][:, 1]
        own = own + jnp.where(low, pltpu.roll(beside, 4, 2), 0.0)
        merged.append(own + jnp.where(high, pltpu.roll(beside, 124, 2), 0.0))
    for c in zr:
        c.wait_recv()
    from_below, from_above = zr_halo[0], zr_halo[1]
    for i in range(8):
        for y_half in range(2):
            place = i * 2 + y_half
            moved = pltpu.roll(from_below, LANES - place, 1) if place else from_below
            total = merged[y_half][i] + jnp.where(lane == 0, moved, 0.0)
            total = total + jnp.where(lane == 124, pltpu.roll(from_above, 124 - place, 1), 0.0)
            rows[i // 2 % 2, i % 2, i // 4, y_half] = total

    row_copies = []
    for side, d in ((0, 1), (1, -1)):
        half = 1 - side
        row_copies.append(Copy(rows.at[1, 0, half], rows_x.at[side], r_send.at[side], r_recv.at[side], (("gx", d),)))
        row_copies.append(Copy(rows.at[0, 1, :, half], rows_y.at[side], r_send.at[2 + side], r_recv.at[2 + side], (("gy", d),)))
        for side_y, d_y in ((0, 1), (1, -1)):
            n = 4 + side * 2 + side_y
            row_copies.append(Copy(
                rows.at[1, 1, half, 1 - side_y], rows_d.at[side, side_y], r_send.at[n], r_recv.at[n],
                (("gx", d), ("gy", d_y)),
            ))
    start(row_copies)
    for c in row_copies:
        c.wait_recv()
    whole = [
        [rows[0, 0, h, y] + rows_x[h, y] + rows_y[y, h] + rows_d[h, y] for y in range(2)] for h in range(2)
    ]
    tiles = jnp.stack([whole[0][0], whole[0][1], whole[1][0], whole[1][1]])
    lows, highs = tiles, pltpu.roll(tiles, 124, 2)
    for b in range(4):
        inside = lax.rem(lane, 2 ** (b + 4))
        takes = (inside >= 2**b) & (inside < 2 ** (b + 1))
        lows = jnp.where(takes, pltpu.roll(lows, LANES - 7 * 2**b, 2), lows)
        highs = jnp.where(takes, pltpu.roll(highs, LANES - 7 * 2**b, 2), highs)
    picks = {0: ((0,), 1), 1: ((0, 1), 0), 2: ((1,), 1)}
    for d_x in range(3):
        for d_y in range(3):
            (halves_x, e_x), (halves_y, e_y) = picks[d_x], picks[d_y]
            low_tile, high_tile = None, None
            for h in halves_x:
                for y in halves_y:
                    n = h * 2 + y
                    low_tile = lows[n] if low_tile is None else low_tile + lows[n]
                    high_tile = highs[n] if high_tile is None else high_tile + highs[n]
            e = e_x * 4 + e_y * 2
            out_row = (d_x * 3 + d_y) * 3
            out_c[out_row:out_row + 1, :] = low_tile[e + 1:e + 2, :16]
            out_c[out_row + 1:out_row + 2, :] = low_tile[e:e + 1, :16] + high_tile[e:e + 1, :16]
            out_c[out_row + 2:out_row + 3, :] = high_tile[e + 1:e + 2, :16]
    out.wait()
    for c in started:
        c.wait_send()


def shards(permeability, well_flags, support_mask):
    f32 = jnp.float32
    vmem = pltpu.VMEM
    dma = pltpu.SemaphoreType.DMA
    any_spec = pl.BlockSpec(memory_space=pltpu.HBM)
    prolongation, coarse = pl.pallas_call(
        kernel,
        out_shape=(
            jax.ShapeDtypeStruct((8, E, E, LANES), f32),
            jax.ShapeDtypeStruct((27, 16), f32),
        ),
        in_specs=[any_spec] * 3,
        out_specs=(any_spec, pl.BlockSpec(memory_space=pltpu.VMEM)),
        scratch_shapes=[
            vmem((10, E, LANES), f32),
            vmem((E, 24, LANES), f32),
            vmem((E, E, LANES), f32),
            vmem((2, E, LANES), f32),
            vmem((2, E, LANES), f32),
            vmem((E, E, LANES), jnp.int32),
            vmem((8, E, E, LANES), jnp.int32),
            vmem((SWEEPS + 1, 8, 10, 24, LANES), f32),
            vmem((SWEEPS + 1, 2, E, LANES), f32),
            vmem((SWEEPS + 1, 2, E, LANES), f32),
            vmem((2, 2, E, E, LANES), f32),
            vmem((2, 2, E, E, LANES), f32),
            vmem((2, 2, E, E, LANES), f32),
            vmem((E, E, LANES), f32),
            vmem((2, 8, E, LANES), f32),
            vmem((4, 2, E, E, LANES), f32),
            vmem((4, 2, E, E, LANES), f32),
            vmem((1024, LANES), f32),
            vmem((2, 2, 2, 2, E, LANES), f32),
            vmem((2, 2, E, LANES), f32),
            vmem((2, 2, E, LANES), f32),
            vmem((2, 2, E, LANES), f32),
            vmem((2, E, LANES), f32),
            vmem((2, E, LANES), f32),
            dma((5,)),
            dma((6,)),
            dma((6,)),
            dma((SWEEPS + 1, 6)),
            dma((SWEEPS + 1, 6)),
            dma((2,)),
            dma((2,)),
            dma((8,)),
            dma((8,)),
            dma((1,)),
        ],
        compiler_params=pltpu.CompilerParams(
            collective_id=0, has_side_effects=True, vmem_limit_bytes=60 * 1024 * 1024
        ),
        name="smooth_and_contract",
    )(permeability, well_flags, support_mask)
    return prolongation, coarse.reshape(3, 3, 3, 1, 1, 16)


def solution(mesh):
    placed = (P(None, "gx", "gy", "gz"), P("gx", "gy", "gz"), P(None, "gx", "gy", "gz"))
    return jax.shard_map(
        shards,
        mesh=mesh,
        in_specs=placed,
        out_specs=(P(None, "gx", "gy", "gz"), P(None, None, None, "gx", "gy", "gz")),
        check_vma=False,
    )
```

profile of v0, /device:TPU:25, one launch (start us, length us, event | category | flops | bytes accessed | tf_op | source)
XLA Modules:
  0.0 43.9 jit_solution(14181133037711705815)
XLA Ops:
  0.6 40.2 %smooth_and_contract.1 = (f32[8,8,8,128]{3,2,1,0:T(8,128)}, f32[27,16]{1,0:T(8,128)}) custom-call(f32[3,8,8,128]{3,2,1,0:T(8,128)} %perm.1, s32[8,8,128]{2,1,0:T(8,128)} %flags.1, s32[8,8,8,128]{3,2,1,0:T(8,128)} %mask.1), custom_call_target="tpu_custom_call" | custom-call | tf_op jit(solution)/shard_map/smooth_and_contract/pallas_call | solution.py:459
  40.9 1.3 %reshape.8 = f32[3,3,3,1,1,16]{5,4,3,2,1,0:T(1,128)} reshape(f32[27,16]{1,0:T(8,128)} %get-tuple-element.5) | data formatting | bytes 3456 | tf_op jit(solution)/shard_map/reshape | solution.py:508
  42.2 1.7 %copy.8 = f32[8,8,8,128]{3,2,1,0:T(8,128)} copy(f32[8,8,8,128]{3,2,1,0:T(8,128)} %get-tuple-element.12) | data formatting | bytes 524288
where the time goes:
time: 44.4 us; the launch traced here: 43.9 us
  Pallas kernels  40.2 us (91%)
  local copies, waits for them, and re-layouts  3 us (7%)
  between operations  0.64 us (1%)
    pallas_call x1, Pallas kernels, shards(): pl.pallas_call(kernel, out_shape=(jax.ShapeDtypeStruct((8, E, E, LANES),...  40.2 us
    unnamed x1, local copies, waits for them, and re-layouts  1.67 us
    reshape x1, local copies, waits for them, and re-layouts, shards(): return (prolongation, coarse.reshape(3, 3, 3, 1, 1, 16))  1.33 us

commit v1 on v0

--- a/solution.py
+++ b/solution.py
@@ -277,13 +277,13 @@
                 weights(x)
                 return carry
 
-            lax.fori_loop(1, 7, prepare, 0)
+            lax.fori_loop(1, 7, prepare, 0, unroll=True)
 
         def inner(x, tiles):
             update(k, x, inner_flow(k, x))
             return pack_z(k + 1, x, tiles)
 
-        tiles = lax.fori_loop(1, 7, inner, (zero, zero))
+        tiles = lax.fori_loop(1, 7, inner, (zero, zero), unroll=True)
         if k > 0:
             for x, side in ((0, 1), (7, 0)):
                 part[1 - side] = (flow_yz(k, x) + flow_x(k, x, side)).reshape(8, E, LANES)
@@ -326,7 +326,7 @@
         pz[:, 1, x] = beside
         return carry
 
-    lax.fori_loop(0, E, split_basis, 0)
+    lax.fori_loop(0, E, split_basis, 0, unroll=True)
     for c in arriving_yz:
         c.wait_recv()
 
@@ -334,7 +334,7 @@
         image(x, inner_flow(SWEEPS, x))
         return carry
 
-    lax.fori_loop(1, 7, inner_image, 0)
+    lax.fori_loop(1, 7, inner_image, 0, unroll=True)
     for x, side in ((0, 1), (7, 0)):
         part[1 - side] = (flow_yz(SWEEPS, x) + flow_x(SWEEPS, x, side)).reshape(8, E, LANES)
 
@@ -357,7 +357,7 @@
                             sums[pl.ds(base, E)] = total
             return carry
 
-        lax.fori_loop(0, 8, body, 0)
+        lax.fori_loop(0, 8, body, 0, unroll=2)
 
     contract(True)
     for c in arriving_x:
@@ -459,11 +459,11 @@
     prolongation, coarse = pl.pallas_call(
         kernel,
         out_shape=(
-            jax.ShapeDtypeStruct((8, E, E, LANES), f32),
-            jax.ShapeDtypeStruct((27, 16), f32),
+            pltpu.VMEM((8, E, E, LANES), f32),
+            pltpu.VMEM((27, 16), f32),
         ),
         in_specs=[any_spec] * 3,
-        out_specs=(any_spec, pl.BlockSpec(memory_space=pltpu.VMEM)),
+        out_specs=(pl.BlockSpec(memory_space=pltpu.VMEM), pl.BlockSpec(memory_space=pltpu.VMEM)),
         scratch_shapes=[
             vmem((10, E, LANES), f32),
             vmem((E, 24, LANES), f32),

time: 44.4 us -> 41 us (0.923)
  local copies, waits for them, and re-layouts: 3 us -> 1.32 us
  Pallas kernels: 40.2 us -> 39 us
    pallas_call x1, Pallas kernels: 40.2 us -> 39 us  [shards(): pl.pallas_call(kernel, out_shape=(pltpu.VMEM((8, E, E, LANES), f32), pltp...]
    unnamed x1, local copies, waits for them, and re-layouts: 1.67 us -> 0.71 us
    reshape x1, local copies, waits for them, and re-layouts: 1.33 us -> 0.62 us  [shards(): return (prolongation, coarse.reshape(3, 3, 3, 1, 1, 16))]
where the time goes in v1:
time: 41 us; the launch traced here: 40.9 us
  Pallas kernels  39 us (95%)
  local copies, waits for them, and re-layouts  1.32 us (3%)
  between operations  0.64 us (2%)
    pallas_call x1, Pallas kernels, shards(): pl.pallas_call(kernel, out_shape=(pltpu.VMEM((8, E, E, LANES), f32), pltp...  39 us

profile of v1, /device:TPU:25, one launch (start us, length us, event | category | flops | bytes accessed | tf_op | source)
XLA Modules:
  0.0 40.9 jit_solution(16405292059709504033)
XLA Ops:
  0.6 39.0 %smooth_and_contract.1 = (f32[8,8,8,128]{3,2,1,0:T(8,128)S(1)}, f32[27,16]{1,0:T(8,128)S(1)}) custom-call(f32[3,8,8,128]{3,2,1,0:T(8,128)} %perm.1, s32[8,8,128]{2,1,0:T(8,128)} %flags.1, s32[8,8,8,128]{3,2,1,0:T(8,128)} %mask.1), custom_call_target="tpu_custom_call" | custom-call | tf_op jit(solution)/shard_map/smooth_and_contract/pallas_call | solution.py:459
  39.6 0.7 %copy.8 = f32[8,8,8,128]{3,2,1,0:T(8,128)} copy(f32[8,8,8,128]{3,2,1,0:T(8,128)S(1)} %get-tuple-element.10) | data formatting | bytes 524288
  40.3 0.6 %reshape.8 = f32[3,3,3,1,1,16]{5,4,3,2,1,0:T(1,128)} reshape(f32[27,16]{1,0:T(8,128)S(1)} %get-tuple-element.5) | data formatting | bytes 3456 | tf_op jit(solution)/shard_map/reshape | solution.py:508

commit v2 on v1

--- a/solution.py
+++ b/solution.py
@@ -24,7 +24,8 @@
     perm, flags, mask, out_p, out_c,
     kx, ky, kz, kz_send, kz_halo, fl, mk, basis, z_send, z_halo,
     vx, vy, vz, negdiag, part, pz, iz, sums, rows, rows_x, rows_y, rows_d, zr_send, zr_halo,
-    load_sem, k_send, k_recv, p_send, p_recv, zr_ssem, zr_rsem, r_send, r_recv, out_sem,
+    faces, face_sums, face_rows, face_rows_y, zf_send, zf_halo,
+    load_sem, k_send, k_recv, p_send, p_recv, r_send, r_recv, out_sem,
 ):
     at = {axis: lax.axis_index(axis) for axis in AXES}
     has = {}
@@ -134,18 +135,36 @@
 
             lax.fori_loop(0, 8 * SWEEPS, clear, 0)
             rows_y[side] = jnp.zeros((2, E, LANES), jnp.float32)
+            face_rows_y[side] = jnp.zeros((2, E, LANES), jnp.float32)
 
         @pl.when(jnp.logical_not(has["gz", d]))
         def _():
             kz_halo[side] = zero
             for k in range(1, SWEEPS + 1):
                 z_halo[k, side] = zero
-            zr_halo[side] = zero
 
         for e in (1, -1):
             @pl.when(jnp.logical_not(has["gx", d] & has["gy", e]))
             def _():
                 rows_d[side, (e + 1) // 2] = zero
+
+    for m_z in (1, -1):
+        side = (1 - m_z) // 2
+        for m_y in (1, 0, -1):
+            near = has["gz", -m_z]
+            if m_y:
+                near = near & has["gy", -m_y]
+
+            @pl.when(jnp.logical_not(near))
+            def _():
+                zf_halo[side, m_y + 1] = zero
+
+            for m_x in (1, 0, -1):
+                there = near & has["gx", -m_x] if m_x else near
+
+                @pl.when(jnp.logical_not(there))
+                def _():
+                    zr_halo[side, m_x + 1, m_y + 1] = zero
 
     for load in loads[:3]:
         load.wait()
@@ -315,11 +334,6 @@
             jnp.where(even, pair[:, 1], pair[:, 0]),
         )
 
-    def image(x, flow):
-        own, beside = split_z(flow * negdiag[x])
-        iz[:, 0, x] = own
-        iz[:, 1, x] = beside
-
     def split_basis(x, carry):
         own, beside = split_z(center_of(SWEEPS, x))
         pz[:, 0, x] = own
@@ -330,100 +344,179 @@
     for c in arriving_yz:
         c.wait_recv()
 
+    def image(x, flow):
+        own, beside = split_z(flow * negdiag[x])
+        iz[:, 0, x] = own
+        iz[:, 1, x] = beside
+
     def inner_image(x, carry):
         image(x, inner_flow(SWEEPS, x))
         return carry
 
     lax.fori_loop(1, 7, inner_image, 0, unroll=True)
     for x, side in ((0, 1), (7, 0)):
-        part[1 - side] = (flow_yz(SWEEPS, x) + flow_x(SWEEPS, x, side)).reshape(8, E, LANES)
-
-    def contract(first):
-        def body(i, carry):
-            half, a_x, a_y = i // 4, lax.rem(i // 2, 2), lax.rem(i, 2)
-            s_xy = lax.rem(a_x + par_x, 2) * 2 + lax.rem(a_y + par_y, 2)
-            planes = [1 + 3 * half + j for j in range(3)] if first else [7 * half]
-            for a_z in range(2):
-                for e_x in range(2):
-                    for e_y in range(2):
-                        u_xy = lax.rem(a_x + e_x + par_x, 2) * 2 + lax.rem(a_y + e_y + par_y, 2)
-                        for e_z in range(2):
-                            e = e_x * 4 + e_y * 2 + e_z
-                            base = pl.multiple_of((i * 2 + a_z) * 64, 64) + e * 8
-                            total = None if first else sums[pl.ds(base, E)]
-                            for x in planes:
-                                term = pz[s_xy, a_z, x] * iz[u_xy, (a_z + e_z) % 2, x]
-                                total = term if total is None else total + term
-                            sums[pl.ds(base, E)] = total
-            return carry
-
-        lax.fori_loop(0, 8, body, 0, unroll=2)
-
-    contract(True)
-    for c in arriving_x:
-        c.wait_recv()
-    for x, side in ((0, 0), (7, 1)):
-        image(x, part[side].reshape(2, 2, 2, E, LANES) + flow_x(SWEEPS, x, side))
-    contract(False)
-
-    quarter = []
-    for y_half in range(2):
-        total = sums[pl.ds(4 * y_half, LANES, stride=8)]
-        for y in range(1, 4):
-            total = total + sums[pl.ds(4 * y_half + y, LANES, stride=8)]
-        total = total.reshape(16, E, LANES)
-        total = total + pltpu.roll(total, 127, 2)
-        total = total + pltpu.roll(total, 126, 2)
-        quarter.append(total.reshape(8, 2, E, LANES))
-    up, down = zero, zero
-    for i in range(8):
+        image(x, flow_yz(SWEEPS, x) + flow_x(SWEEPS, x, side))
+
+    def pair_of(a_x, a_y):
+        return lax.rem(a_x + par_x, 2) * 2 + lax.rem(a_y + par_y, 2)
+
+    def contract(i, carry):
+        half, a_x, a_y = i // 4, lax.rem(i // 2, 2), lax.rem(i, 2)
+        for a_z in range(2):
+            for e in range(8):
+                u_xy = pair_of(a_x + e // 4, a_y + e // 2 % 2)
+                total = None
+                for j in range(4):
+                    x = 4 * half + j
+                    term = pz[pair_of(a_x, a_y), a_z, x] * iz[u_xy, (a_z + e) % 2, x]
+                    total = term if total is None else total + term
+                sums[pl.ds(pl.multiple_of((i * 2 + a_z) * 64, 64) + e * 8, E)] = total
+        return carry
+
+    lax.fori_loop(0, 8, contract, 0, unroll=2)
+
+    def halves(ref, count):
+        results = []
         for y_half in range(2):
-            place = i * 2 + y_half
-            beside = quarter[y_half][i, 1]
+            total = ref[pl.ds(4 * y_half, count * 8, stride=8)]
+            for y in range(1, 4):
+                total = total + ref[pl.ds(4 * y_half + y, count * 8, stride=8)]
+            total = total.reshape(count, E, LANES)
+            total = total + pltpu.roll(total, 127, 2)
+            total = total + pltpu.roll(total, 126, 2)
+            results.append(total.reshape(count // 2, 2, E, LANES))
+        return results
+
+    low = (lax.rem(lane, E) == 0) & (lane != 0)
+    high = (lax.rem(lane, E) == 4) & (lane != 124)
+
+    def merge_z(pair):
+        own, beside = pair[:, 0], pair[:, 1]
+        own = own + jnp.where(low, pltpu.roll(beside, 4, 2), 0.0)
+        return own + jnp.where(high, pltpu.roll(beside, 124, 2), 0.0)
+
+    def pack_rows(entries):
+        up, down = zero, zero
+        for place, beside in entries:
             up = jnp.where(lane == place, pltpu.roll(beside, place + 4, 1), up)
             moved = pltpu.roll(beside, place, 1) if place else beside
             down = jnp.where(lane == place, moved, down)
-    zr_send[0], zr_send[1] = up, down
-    zr = [
-        Copy(zr_send.at[0], zr_halo.at[0], zr_ssem.at[0], zr_rsem.at[0], (("gz", 1),)),
-        Copy(zr_send.at[1], zr_halo.at[1], zr_ssem.at[1], zr_rsem.at[1], (("gz", -1),)),
-    ]
-    start(zr)
-    low = (lax.rem(lane, E) == 0) & (lane != 0)
-    high = (lax.rem(lane, E) == 4) & (lane != 124)
-    merged = []
+        return up, down
+
+    row_copies = []
+
+    def move_rows(src, dst, moves):
+        n = len(row_copies)
+        row_copies.append(Copy(src, dst, r_send.at[n], r_recv.at[n], tuple(m for m in moves if m[1])))
+
+    quarter = halves(sums, 16)
+    entries = []
+    for i in range(8):
+        half, a_x, a_y = i // 4, i // 2 % 2, i % 2
+        for y_half in range(2):
+            place = (a_x * 2 + a_y) * 32 + (half ^ a_x) * 2 + (y_half ^ a_y)
+            entries.append((place, quarter[y_half][i, 1]))
+    zr_send[0], zr_send[1] = pack_rows(entries)
+    order = [(m_x, m_y) for m_x in (1, -1, 0) for m_y in (1, -1, 0)]
+    for side, m_z in ((0, 1), (1, -1)):
+        for m_x, m_y in order:
+            move_rows(
+                zr_send.at[side], zr_halo.at[side, m_x + 1, m_y + 1],
+                (("gx", m_x), ("gy", m_y), ("gz", m_z)),
+            )
+    start(row_copies)
     for y_half in range(2):
-        own, beside = quarter[y_half][:, 0], quarter[y_half][:, 1]
-        own = own + jnp.where(low, pltpu.roll(beside, 4, 2), 0.0)
-        merged.append(own + jnp.where(high, pltpu.roll(beside, 124, 2), 0.0))
-    for c in zr:
+        merged = merge_z(quarter[y_half])
+        for i in range(8):
+            rows[i // 2 % 2, i % 2, i // 4, y_half] = merged[i]
+    first = len(row_copies)
+    for side, d in ((0, 1), (1, -1)):
+        for side_y, d_y in ((0, 1), (1, -1)):
+            move_rows(
+                rows.at[1, 1, 1 - side, 1 - side_y], rows_d.at[side, side_y], (("gx", d), ("gy", d_y))
+            )
+    for side, d in ((0, 1), (1, -1)):
+        move_rows(rows.at[1, 0, 1 - side], rows_x.at[side], (("gx", d),))
+        move_rows(rows.at[0, 1, :, 1 - side], rows_y.at[side], (("gy", d),))
+    start(row_copies[first:])
+    first = len(row_copies)
+
+    for c in arriving_x:
         c.wait_recv()
-    from_below, from_above = zr_halo[0], zr_halo[1]
-    for i in range(8):
+    for side in range(2):
+        x = 7 * side
+        weight = vx[0, side, x] * negdiag[x]
+        for n, plane in enumerate((x + 1, 9 * side)):
+            own, beside = split_z(basis[SWEEPS, :, plane, 8:16])
+            faces[side, n, 0, :, 0] = own
+            faces[side, n, 0, :, 1] = beside
+            faces[side, n, 1, :, 0] = own * weight
+            faces[side, n, 1, :, 1] = beside * weight
+
+    def contract_faces(i, carry):
+        side, a_y = i // 2, lax.rem(i, 2)
+        s_xy = pair_of(0, a_y)
+        for a_z in range(2):
+            for e in range(8):
+                u_xy = pair_of(e // 4, a_y + e // 2 % 2)
+                u_z = (a_z + e) % 2
+                total = faces[side, 0, 0, s_xy, a_z] * faces[side, 1, 1, u_xy, u_z]
+                total = total + faces[side, 1, 0, s_xy, a_z] * faces[side, 0, 1, u_xy, u_z]
+                face_sums[pl.ds(pl.multiple_of((i * 2 + a_z) * 64, 64) + e * 8, E)] = total
+        return carry
+
+    lax.fori_loop(0, 4, contract_faces, 0, unroll=True)
+    quarter = halves(face_sums, 8)
+    entries = []
+    for i in range(4):
+        half, a_y = i // 2, i % 2
         for y_half in range(2):
-            place = i * 2 + y_half
-            moved = pltpu.roll(from_below, LANES - place, 1) if place else from_below
-            total = merged[y_half][i] + jnp.where(lane == 0, moved, 0.0)
-            total = total + jnp.where(lane == 124, pltpu.roll(from_above, 124 - place, 1), 0.0)
-            rows[i // 2 % 2, i % 2, i // 4, y_half] = total
-
-    row_copies = []
+            entries.append((a_y * 32 + half * 2 + (y_half ^ a_y), quarter[y_half][i, 1]))
+    zf_send[0], zf_send[1] = pack_rows(entries)
+    for side, m_z in ((0, 1), (1, -1)):
+        for m_y in (1, -1, 0):
+            move_rows(zf_send.at[side], zf_halo.at[side, m_y + 1], (("gy", m_y), ("gz", m_z)))
+    start(row_copies[first:])
+    first = len(row_copies)
+    face_own = []
+    for y_half in range(2):
+        merged = merge_z(quarter[y_half])
+        face_own.append((merged[0], merged[2]))
+        face_rows[y_half, 0], face_rows[y_half, 1] = merged[1], merged[3]
     for side, d in ((0, 1), (1, -1)):
-        half = 1 - side
-        row_copies.append(Copy(rows.at[1, 0, half], rows_x.at[side], r_send.at[side], r_recv.at[side], (("gx", d),)))
-        row_copies.append(Copy(rows.at[0, 1, :, half], rows_y.at[side], r_send.at[2 + side], r_recv.at[2 + side], (("gy", d),)))
-        for side_y, d_y in ((0, 1), (1, -1)):
-            n = 4 + side * 2 + side_y
-            row_copies.append(Copy(
-                rows.at[1, 1, half, 1 - side_y], rows_d.at[side, side_y], r_send.at[n], r_recv.at[n],
-                (("gx", d), ("gy", d_y)),
-            ))
-    start(row_copies)
+        move_rows(face_rows.at[1 - side], face_rows_y.at[side], (("gy", d),))
+    start(row_copies[first:])
+
     for c in row_copies:
         c.wait_recv()
     whole = [
-        [rows[0, 0, h, y] + rows_x[h, y] + rows_y[y, h] + rows_d[h, y] for y in range(2)] for h in range(2)
+        [
+            rows[0, 0, h, y] + rows_x[h, y] + rows_y[y, h] + rows_d[h, y] + face_own[y][h] + face_rows_y[y, h]
+            for y in range(2)
+        ]
+        for h in range(2)
     ]
+    for side in range(2):
+        packed = zero
+        for m_x, m_y in order:
+            inside = lane - 32 * (2 * abs(m_x) + abs(m_y))
+            takes = (inside >= 0) & (inside < 4)
+            if m_x:
+                takes = takes & (inside // 2 == (1 - m_x) // 2)
+            if m_y:
+                takes = takes & (lax.rem(inside, 2) == (1 - m_y) // 2)
+            value = zr_halo[side, m_x + 1, m_y + 1]
+            if m_x == 0:
+                value = value + zf_halo[side, m_y + 1]
+            packed = packed + jnp.where(takes, value, 0.0)
+        packed = packed + pltpu.roll(packed, 64, 1)
+        packed = packed + pltpu.roll(packed, 32, 1)
+        target = 124 * side
+        for h in range(2):
+            for y in range(2):
+                shift = (target - (h * 2 + y)) % LANES
+                moved = pltpu.roll(packed, shift, 1) if shift else packed
+                whole[h][y] = whole[h][y] + jnp.where(lane == target, moved, 0.0)
     tiles = jnp.stack([whole[0][0], whole[0][1], whole[1][0], whole[1][1]])
     lows, highs = tiles, pltpu.roll(tiles, 124, 2)
     for b in range(4):
@@ -488,16 +581,20 @@
             vmem((2, 2, E, LANES), f32),
             vmem((2, 2, E, LANES), f32),
             vmem((2, E, LANES), f32),
+            vmem((2, 3, 3, E, LANES), f32),
+            vmem((2, 2, 2, 4, 2, E, LANES), f32),
+            vmem((512, LANES), f32),
+            vmem((2, 2, E, LANES), f32),
+            vmem((2, 2, E, LANES), f32),
             vmem((2, E, LANES), f32),
+            vmem((2, 3, E, LANES), f32),
             dma((5,)),
             dma((6,)),
             dma((6,)),
             dma((SWEEPS + 1, 6)),
             dma((SWEEPS + 1, 6)),
-            dma((2,)),
-            dma((2,)),
-            dma((8,)),
-            dma((8,)),
+            dma((34,)),
+            dma((34,)),
             dma((1,)),
         ],
         compiler_params=pltpu.CompilerParams(

time: 41 us -> 38.7 us (0.944)
  Pallas kernels: 39 us -> 36.6 us
    pallas_call x1, Pallas kernels: 39 us -> 36.6 us  [shards(): pl.pallas_call(kernel, out_shape=(pltpu.VMEM((8, E, E, LANES), f32), pltp...]
where the time goes in v2:
time: 38.7 us; the launch traced here: 38.6 us
  Pallas kernels  36.6 us (95%)
  local copies, waits for them, and re-layouts  1.32 us (3%)
  between operations  0.64 us (2%)
    pallas_call x1, Pallas kernels, shards(): pl.pallas_call(kernel, out_shape=(pltpu.VMEM((8, E, E, LANES), f32), pltp...  36.6 us

profile of v2, /device:TPU:25, one launch (start us, length us, event | category | flops | bytes accessed | tf_op | source)
XLA Modules:
  0.0 38.6 jit_solution(6231973229533685805)
XLA Ops:
  0.6 36.6 %smooth_and_contract.1 = (f32[8,8,8,128]{3,2,1,0:T(8,128)S(1)}, f32[27,16]{1,0:T(8,128)S(1)}) custom-call(f32[3,8,8,128]{3,2,1,0:T(8,128)} %perm.1, s32[8,8,128]{2,1,0:T(8,128)} %flags.1, s32[8,8,8,128]{3,2,1,0:T(8,128)} %mask.1), custom_call_target="tpu_custom_call" | custom-call | tf_op jit(solution)/shard_map/smooth_and_contract/pallas_call | solution.py:552
  37.3 0.7 %copy.8 = f32[8,8,8,128]{3,2,1,0:T(8,128)} copy(f32[8,8,8,128]{3,2,1,0:T(8,128)S(1)} %get-tuple-element.10) | data formatting | bytes 524288
  38.0 0.6 %reshape.8 = f32[3,3,3,1,1,16]{5,4,3,2,1,0:T(1,128)} reshape(f32[27,16]{1,0:T(8,128)S(1)} %get-tuple-element.5) | data formatting | bytes 3456 | tf_op jit(solution)/shard_map/reshape | solution.py:605

commit v3 on v2

--- a/solution.py
+++ b/solution.py
@@ -24,8 +24,8 @@
     perm, flags, mask, out_p, out_c,
     kx, ky, kz, kz_send, kz_halo, fl, mk, basis, z_send, z_halo,
     vx, vy, vz, negdiag, part, pz, iz, sums, rows, rows_x, rows_y, rows_d, zr_send, zr_halo,
-    faces, face_sums, face_rows, face_rows_y, zf_send, zf_halo,
-    load_sem, k_send, k_recv, p_send, p_recv, r_send, r_recv, out_sem,
+    faces, face_sums, face_rows, face_rows_y, zf_send, zf_halo, a_send, a_halo, mask_halo, part_halo, halo_vx,
+    load_sem, k_send, k_recv, p_send, p_recv, r_send, r_recv, h_send, h_recv, out_sem,
 ):
     at = {axis: lax.axis_index(axis) for axis in AXES}
     has = {}
@@ -109,7 +109,8 @@
     slot = lane // E
     hot_xy = (slot // 4 == par_x) & (lax.rem(slot // 2, 2) == par_y)
     for side in range(2):
-        z_halo[0, side] = jnp.where(hot_xy & (lax.rem(slot, 2) == 1 - side), 1.0, 0.0)
+        for group in range(2):
+            z_halo[0, group, side] = jnp.where(hot_xy & (lax.rem(slot, 2) == 1 - side), 1.0, 0.0)
 
     zero = jnp.zeros((E, LANES), jnp.float32)
     for d, k_plane in ((-1, 0), (1, 9)):
@@ -118,6 +119,9 @@
         @pl.when(jnp.logical_not(has["gx", d]))
         def _():
             kx[k_plane] = zero
+            a_halo[side] = jnp.ones((3, E, LANES), jnp.float32)
+            mask_halo[side] = jnp.zeros((8, E, LANES), jnp.int32)
+            part_halo[side] = jnp.zeros((8, E, LANES), jnp.float32)
             for k in range(1, SWEEPS + 1):
                 basis[k, :, k_plane, 8:16] = jnp.zeros((8, E, LANES), jnp.float32)
             rows_x[side] = jnp.zeros((2, E, LANES), jnp.float32)
@@ -141,7 +145,8 @@
         def _():
             kz_halo[side] = zero
             for k in range(1, SWEEPS + 1):
-                z_halo[k, side] = zero
+                z_halo[k, 0, side] = zero
+                z_halo[k, 1, side] = zero
 
         for e in (1, -1):
             @pl.when(jnp.logical_not(has["gx", d] & has["gy", e]))
@@ -188,10 +193,20 @@
     ]
     start(k_x)
     start(k_yz)
-
-    def weights(x):
-        here = kx[x + 1]
-        t_x = (harmonic(kx[x], here), harmonic(here, kx[x + 2]))
+    for load in loads[3:]:
+        load.wait()
+    h_copies = []
+    for src, dst in ((mk, mask_halo), (a_send, a_halo), (part, part_halo)):
+        for side, d in ((0, -1), (1, 1)):
+            n = len(h_copies)
+            if src is mk:
+                block = mk.at[:, 7 * side]
+            else:
+                block = src.at[2, side] if src is part else src.at[side]
+            h_copies.append(Copy(block, dst.at[1 - side], h_send.at[n], h_recv.at[n], (("gx", d),)))
+    start(h_copies[:2])
+
+    def faces_yz(x):
         here = ky[x, 8:16]
         t_y = (harmonic(ky[x, 7:15], here), harmonic(here, ky[x, 9:17]))
         here = kz[x]
@@ -201,7 +216,56 @@
         after = jnp.where(
             lane == 127, pltpu.roll(kz_halo[1], 127 - x, 1), pltpu.roll(here, 127, 1)
         )
-        t_z = (harmonic(before, here), harmonic(here, after))
+        return t_y, (harmonic(before, here), harmonic(here, after))
+
+    def outer_plane(side):
+        x = 7 * side
+        t_x = harmonic(kx[x + 1 - side], kx[x + 2 - side])
+        t_y, t_z = faces_yz(x)
+        total = t_x + t_y[0] + t_y[1] + t_z[0] + t_z[1]
+        a_send[side, 0] = total + WELL * fl[x].astype(jnp.float32)
+        a_send[side, 1] = jnp.where(row == 0, t_y[0], jnp.where(row == 7, t_y[1], 0.0))
+        place = lax.rem(lane, E)
+        a_send[side, 2] = jnp.where(place == 0, t_z[0], jnp.where(place == 7, t_z[1], 0.0))
+
+    def first_halo(side):
+        plane, away = 9 * side, 1 - par_x
+        t_x = harmonic(kx[8 * side], kx[8 * side + 1])
+        scale = STEP / (a_halo[side, 0] + t_x)
+        halo_vx[side] = t_x * scale
+
+        def support(b_x, b_y, own):
+            n = 4 * b_x + 2 * b_y
+            low, high = mask_halo[side, n], mask_halo[side, n + 1]
+            pair = (low, high) if own else (high, low)
+            return jnp.where(even, *pair).astype(jnp.float32)
+
+        u_x = support(par_x, par_y, True) * (t_x * scale)
+        u_y = support(away, 1 - par_y, True) * (a_halo[side, 1] * scale)
+        u_z = support(away, par_y, False) * (a_halo[side, 2] * scale)
+        own = 1.0 - (u_x + u_y + u_z)
+
+        def put(b_x, b_y, own_z, beside_z):
+            n = 4 * b_x + 2 * b_y
+            basis[1, n, plane, 8:16] = jnp.where(even, own_z, beside_z)
+            basis[1, n + 1, plane, 8:16] = jnp.where(even, beside_z, own_z)
+
+        put(away, par_y, own, u_z)
+        put(par_x, par_y, u_x, zero)
+        put(away, 1 - par_y, u_y, zero)
+        put(par_x, 1 - par_y, zero, zero)
+
+    def third_halo(side):
+        plane = 9 * side
+        flow = part_halo[side] + halo_vx[side] * basis[2, :, 1 + 7 * side, 8:16]
+        center = basis[2, :, plane, 8:16]
+        change = mask_halo[side].astype(jnp.float32) * flow
+        basis[3, :, plane, 8:16] = center + change - center * jnp.sum(change, axis=0)
+
+    def weights(x):
+        here = kx[x + 1]
+        t_x = (harmonic(kx[x], here), harmonic(here, kx[x + 2]))
+        t_y, t_z = faces_yz(x)
         diagonal = t_x[0] + t_x[1] + t_y[0] + t_y[1] + t_z[0] + t_z[1]
         diagonal = diagonal + WELL * fl[x].astype(jnp.float32)
         negdiag[x] = -1.5 * diagonal
@@ -224,14 +288,14 @@
         near = basis[k, :, x + 2 * side, 8:16].reshape(2, 2, 2, E, LANES)
         return vx[:, side, x][:, None, None] * near
 
-    def flow_yz(k, x):
+    def flow_yz(k, x, group):
         center = basis[k, :, x + 1, 8:16]
         total = -STEP * center.reshape(2, 2, 2, E, LANES)
         for side in range(2):
             near = basis[k, :, x + 1, 7 + 2 * side:15 + 2 * side].reshape(2, 2, 2, E, LANES)
             total = total + vy[:, side, x][None, :, None] * near
             edge = lane == (0, 127)[side]
-            halo = z_halo[k, side]
+            halo = z_halo[k, group, side]
             moved = []
             for s in range(8):
                 place = s * 8 + x
@@ -267,60 +331,87 @@
     def copies(k):
         ref = basis.at[k]
         own = pl.ds(8, E)
-        planes = pl.ds(1, E)
-        sems = [(p_send.at[k, i], p_recv.at[k, i]) for i in range(6)]
+        sems = [(p_send.at[k, i], p_recv.at[k, i]) for i in range(12)]
         x = [
             Copy(ref.at[:, 8, own], ref.at[:, 0, own], *sems[0], (("gx", 1),)),
             Copy(ref.at[:, 1, own], ref.at[:, 9, own], *sems[1], (("gx", -1),)),
-        ]
-        yz = [
-            Copy(ref.at[:, planes, pl.ds(15, 1)], ref.at[:, planes, pl.ds(7, 1)], *sems[2], (("gy", 1),)),
-            Copy(ref.at[:, planes, pl.ds(8, 1)], ref.at[:, planes, pl.ds(16, 1)], *sems[3], (("gy", -1),)),
-            Copy(z_send.at[k, 0], z_halo.at[k, 0], *sems[4], (("gz", 1),)),
-            Copy(z_send.at[k, 1], z_halo.at[k, 1], *sems[5], (("gz", -1),)),
-        ]
-        return x, yz
-
-    def inner_flow(k, x):
-        return flow_yz(k, x) + flow_x(k, x, 0) + flow_x(k, x, 1)
-
-    arriving_x, arriving_yz = k_x, k_yz
+        ] if k % 2 == 0 else []
+        yz = []
+        for group in range(2):
+            part_yz = []
+            for n, planes in enumerate((pl.ds(2, 6),) if group == 0 else (pl.ds(1, 1), pl.ds(8, 1))):
+                at_sem = 2 + 2 * group + 2 * n
+                for side, (a, b, d) in enumerate(((15, 7, 1), (8, 16, -1))):
+                    part_yz.append(Copy(
+                        ref.at[:, planes, pl.ds(a, 1)], ref.at[:, planes, pl.ds(b, 1)],
+                        *sems[at_sem + side], (("gy", d),),
+                    ))
+            for side, d in ((0, 1), (1, -1)):
+                part_yz.append(Copy(
+                    z_send.at[k, group, side], z_halo.at[k, group, side],
+                    *sems[8 + 2 * group + side], (("gz", d),),
+                ))
+            yz.append(part_yz)
+        return x, yz[0], yz[1]
+
+    def inner_flow(k, x, group=0):
+        return flow_yz(k, x, group) + flow_x(k, x, 0) + flow_x(k, x, 1)
+
+    arriving_x = []
     for k in range(SWEEPS):
-        for c in arriving_yz:
-            c.wait_recv()
+        next_x, next_inner, next_outer = copies(k + 1)
         if k == 0:
-            for load in loads[3:]:
-                load.wait()
+            for c in k_yz:
+                c.wait_recv()
+            for side in range(2):
+                outer_plane(side)
+            start(h_copies[2:4])
 
             def prepare(x, carry):
                 weights(x)
                 return carry
 
             lax.fori_loop(1, 7, prepare, 0, unroll=True)
+        else:
+            for c in arriving_inner:
+                c.wait_recv()
 
         def inner(x, tiles):
             update(k, x, inner_flow(k, x))
             return pack_z(k + 1, x, tiles)
 
         tiles = lax.fori_loop(1, 7, inner, (zero, zero), unroll=True)
+        z_send[k + 1, 0, 0], z_send[k + 1, 0, 1] = tiles
+        start(next_inner)
         if k > 0:
+            for c in arriving_outer:
+                c.wait_recv()
             for x, side in ((0, 1), (7, 0)):
-                part[1 - side] = (flow_yz(k, x) + flow_x(k, x, side)).reshape(8, E, LANES)
-        for c in arriving_x:
+                part[k, 1 - side] = (flow_yz(k, x, 1) + flow_x(k, x, side)).reshape(8, E, LANES)
+            if k == 2:
+                start(h_copies[4:])
+        for c in (k_x, h_copies[:4], arriving_x, h_copies[4:])[k]:
             c.wait_recv()
-        arriving_x, arriving_yz = copies(k + 1)
+        for side in range(2):
+            if k == 1:
+                first_halo(side)
+            if k == 3:
+                third_halo(side)
         for x, side in ((0, 0), (7, 1)):
             if k == 0:
                 weights(x)
-                flow = inner_flow(k, x)
+                flow = inner_flow(k, x, 1)
             else:
-                flow = part[side].reshape(2, 2, 2, E, LANES) + flow_x(k, x, side)
+                flow = part[k, side].reshape(2, 2, 2, E, LANES) + flow_x(k, x, side)
             update(k, x, flow)
-        start(arriving_x)
+        if k % 2:
+            start(next_x)
+        tiles = (zero, zero)
         for x in (0, 7):
             tiles = pack_z(k + 1, x, tiles)
-        z_send[k + 1, 0], z_send[k + 1, 1] = tiles
-        start(arriving_yz)
+        z_send[k + 1, 1, 0], z_send[k + 1, 1, 1] = tiles
+        start(next_outer)
+        arriving_x, arriving_inner, arriving_outer = next_x, next_inner, next_outer
 
     out = pltpu.make_async_copy(
         basis.at[SWEEPS, :, pl.ds(1, E), pl.ds(8, E)], out_p, out_sem.at[0]
@@ -341,7 +432,7 @@
         return carry
 
     lax.fori_loop(0, E, split_basis, 0, unroll=True)
-    for c in arriving_yz:
+    for c in arriving_inner + arriving_outer:
         c.wait_recv()
 
     def image(x, flow):
@@ -355,7 +446,7 @@
 
     lax.fori_loop(1, 7, inner_image, 0, unroll=True)
     for x, side in ((0, 1), (7, 0)):
-        image(x, flow_yz(SWEEPS, x) + flow_x(SWEEPS, x, side))
+        image(x, flow_yz(SWEEPS, x, 1) + flow_x(SWEEPS, x, side))
 
     def pair_of(a_x, a_y):
         return lax.rem(a_x + par_x, 2) * 2 + lax.rem(a_y + par_y, 2)
@@ -566,13 +657,13 @@
             vmem((E, E, LANES), jnp.int32),
             vmem((8, E, E, LANES), jnp.int32),
             vmem((SWEEPS + 1, 8, 10, 24, LANES), f32),
-            vmem((SWEEPS + 1, 2, E, LANES), f32),
-            vmem((SWEEPS + 1, 2, E, LANES), f32),
+            vmem((SWEEPS + 1, 2, 2, E, LANES), f32),
+            vmem((SWEEPS + 1, 2, 2, E, LANES), f32),
             vmem((2, 2, E, E, LANES), f32),
             vmem((2, 2, E, E, LANES), f32),
             vmem((2, 2, E, E, LANES), f32),
             vmem((E, E, LANES), f32),
-            vmem((2, 8, E, LANES), f32),
+            vmem((SWEEPS, 2, 8, E, LANES), f32),
             vmem((4, 2, E, E, LANES), f32),
             vmem((4, 2, E, E, LANES), f32),
             vmem((1024, LANES), f32),
@@ -588,13 +679,20 @@
             vmem((2, 2, E, LANES), f32),
             vmem((2, E, LANES), f32),
             vmem((2, 3, E, LANES), f32),
+            vmem((2, 3, E, LANES), f32),
+            vmem((2, 3, E, LANES), f32),
+            vmem((2, 8, E, LANES), jnp.int32),
+            vmem((2, 8, E, LANES), f32),
+            vmem((2, E, LANES), f32),
             dma((5,)),
             dma((6,)),
             dma((6,)),
-            dma((SWEEPS + 1, 6)),
-            dma((SWEEPS + 1, 6)),
+            dma((SWEEPS + 1, 12)),
+            dma((SWEEPS + 1, 12)),
             dma((34,)),
             dma((34,)),
+            dma((6,)),
+            dma((6,)),
             dma((1,)),
         ],
         compiler_params=pltpu.CompilerParams(

time: 38.7 us -> 36.6 us (0.946)
  Pallas kernels: 36.6 us -> 34.5 us
    pallas_call x1, Pallas kernels: 36.6 us -> 34.5 us  [shards(): pl.pallas_call(kernel, out_shape=(pltpu.VMEM((8, E, E, LANES), f32), pltp...]
where the time goes in v3:
time: 36.6 us; the launch traced here: 36.5 us
  Pallas kernels  34.5 us (94%)
  local copies, waits for them, and re-layouts  1.32 us (4%)
  between operations  0.64 us (2%)
    pallas_call x1, Pallas kernels, shards(): pl.pallas_call(kernel, out_shape=(pltpu.VMEM((8, E, E, LANES), f32), pltp...  34.5 us

profile of v3, /device:TPU:25, one launch (start us, length us, event | category | flops | bytes accessed | tf_op | source)
XLA Modules:
  0.0 36.5 jit_solution(5123895576889197864)
XLA Ops:
  0.6 34.5 %smooth_and_contract.1 = (f32[8,8,8,128]{3,2,1,0:T(8,128)S(1)}, f32[27,16]{1,0:T(8,128)S(1)}) custom-call(f32[3,8,8,128]{3,2,1,0:T(8,128)} %perm.1, s32[8,8,128]{2,1,0:T(8,128)} %flags.1, s32[8,8,8,128]{3,2,1,0:T(8,128)} %mask.1), custom_call_target="tpu_custom_call" | custom-call | tf_op jit(solution)/shard_map/smooth_and_contract/pallas_call | solution.py:643
  35.2 0.7 %copy.8 = f32[8,8,8,128]{3,2,1,0:T(8,128)} copy(f32[8,8,8,128]{3,2,1,0:T(8,128)S(1)} %get-tuple-element.10) | data formatting | bytes 524288
  35.9 0.6 %reshape.8 = f32[3,3,3,1,1,16]{5,4,3,2,1,0:T(1,128)} reshape(f32[27,16]{1,0:T(8,128)S(1)} %get-tuple-element.5) | data formatting | bytes 3456 | tf_op jit(solution)/shard_map/reshape | solution.py:703

commit v4 on v3

--- a/solution.py
+++ b/solution.py
@@ -24,7 +24,7 @@
     perm, flags, mask, out_p, out_c,
     kx, ky, kz, kz_send, kz_halo, fl, mk, basis, z_send, z_halo,
     vx, vy, vz, negdiag, part, pz, iz, sums, rows, rows_x, rows_y, rows_d, zr_send, zr_halo,
-    faces, face_sums, face_rows, face_rows_y, zf_send, zf_halo, a_send, a_halo, mask_halo, part_halo, halo_vx,
+    faces, face_sums, face_rows, face_rows_y, zf_send, zf_halo, a_send, a_halo, mask_halo, part_halo, halo_vx, t_yz, near_sum,
     load_sem, k_send, k_recv, p_send, p_recv, r_send, r_recv, h_send, h_recv, out_sem,
 ):
     at = {axis: lax.axis_index(axis) for axis in AXES}
@@ -92,25 +92,6 @@
         for c in copies:
             c.start()
         started.extend(copies)
-
-    def fill(i, carry):
-        s, x = i // 10, lax.rem(i, 10)
-        bx, by, bz = s // 4, lax.rem(s // 2, 2), lax.rem(s, 2)
-        block_x = jnp.where((x == 0) | (x == 9), 1 - par_x, par_x)
-        hot_x = (bx == block_x).astype(jnp.float32)
-        own_y = (by == par_y).astype(jnp.float32)
-        hot_z = jnp.where(lax.rem(lane // E, 2) == bz, hot_x, 0.0)
-        basis[0, s, x, 0:8] = hot_z * (1.0 - own_y)
-        basis[0, s, x, 8:16] = hot_z * own_y
-        basis[0, s, x, 16:24] = hot_z * (1.0 - own_y)
-        return carry
-
-    lax.fori_loop(0, 80, fill, 0)
-    slot = lane // E
-    hot_xy = (slot // 4 == par_x) & (lax.rem(slot // 2, 2) == par_y)
-    for side in range(2):
-        for group in range(2):
-            z_halo[0, group, side] = jnp.where(hot_xy & (lax.rem(slot, 2) == 1 - side), 1.0, 0.0)
 
     zero = jnp.zeros((E, LANES), jnp.float32)
     for d, k_plane in ((-1, 0), (1, 9)):
@@ -218,42 +199,48 @@
         )
         return t_y, (harmonic(before, here), harmonic(here, after))
 
-    def outer_plane(side):
-        x = 7 * side
-        t_x = harmonic(kx[x + 1 - side], kx[x + 2 - side])
+    def prepare(x, inner_x):
         t_y, t_z = faces_yz(x)
-        total = t_x + t_y[0] + t_y[1] + t_z[0] + t_z[1]
-        a_send[side, 0] = total + WELL * fl[x].astype(jnp.float32)
-        a_send[side, 1] = jnp.where(row == 0, t_y[0], jnp.where(row == 7, t_y[1], 0.0))
+        for n in range(2):
+            t_yz[x, n] = t_y[n]
+            t_yz[x, 2 + n] = t_z[n]
+        total = t_y[0] + t_y[1] + t_z[0] + t_z[1]
+        for n in inner_x:
+            total = total + harmonic(kx[x + n], kx[x + n + 1])
+        total = total + WELL * fl[x].astype(jnp.float32)
+        near_sum[x] = total
         place = lax.rem(lane, E)
-        a_send[side, 2] = jnp.where(place == 0, t_z[0], jnp.where(place == 7, t_z[1], 0.0))
-
-    def first_halo(side):
-        plane, away = 9 * side, 1 - par_x
-        t_x = harmonic(kx[8 * side], kx[8 * side + 1])
-        scale = STEP / (a_halo[side, 0] + t_x)
-        halo_vx[side] = t_x * scale
-
+        cross_y = jnp.where(row == 0, t_y[0], jnp.where(row == 7, t_y[1], 0.0))
+        cross_z = jnp.where(place == 0, t_z[0], jnp.where(place == 7, t_z[1], 0.0))
+        return total, cross_y, cross_z
+
+    def first_values(masks, plane, own_x, scale, t_x, t_y, t_z):
         def support(b_x, b_y, own):
             n = 4 * b_x + 2 * b_y
-            low, high = mask_halo[side, n], mask_halo[side, n + 1]
-            pair = (low, high) if own else (high, low)
+            pair = (masks(n), masks(n + 1)) if own else (masks(n + 1), masks(n))
             return jnp.where(even, *pair).astype(jnp.float32)
 
-        u_x = support(par_x, par_y, True) * (t_x * scale)
-        u_y = support(away, 1 - par_y, True) * (a_halo[side, 1] * scale)
-        u_z = support(away, par_y, False) * (a_halo[side, 2] * scale)
-        own = 1.0 - (u_x + u_y + u_z)
+        u_y = support(own_x, 1 - par_y, True) * (t_y * scale)
+        u_z = support(own_x, par_y, False) * (t_z * scale)
+        u_x = zero if t_x is None else support(1 - own_x, par_y, True) * (t_x * scale)
 
         def put(b_x, b_y, own_z, beside_z):
             n = 4 * b_x + 2 * b_y
             basis[1, n, plane, 8:16] = jnp.where(even, own_z, beside_z)
             basis[1, n + 1, plane, 8:16] = jnp.where(even, beside_z, own_z)
 
-        put(away, par_y, own, u_z)
-        put(par_x, par_y, u_x, zero)
-        put(away, 1 - par_y, u_y, zero)
-        put(par_x, 1 - par_y, zero, zero)
+        put(own_x, par_y, 1.0 - (u_x + u_y + u_z), u_z)
+        put(1 - own_x, par_y, u_x, zero)
+        put(own_x, 1 - par_y, u_y, zero)
+        put(1 - own_x, 1 - par_y, zero, zero)
+
+    def first_halo(side):
+        t_x = harmonic(kx[8 * side], kx[8 * side + 1])
+        scale = STEP / (a_halo[side, 0] + t_x)
+        halo_vx[side] = t_x * scale
+        first_values(
+            lambda n: mask_halo[side, n], 9 * side, 1 - par_x, scale, t_x, a_halo[side, 1], a_halo[side, 2]
+        )
 
     def third_halo(side):
         plane = 9 * side
@@ -265,9 +252,8 @@
     def weights(x):
         here = kx[x + 1]
         t_x = (harmonic(kx[x], here), harmonic(here, kx[x + 2]))
-        t_y, t_z = faces_yz(x)
-        diagonal = t_x[0] + t_x[1] + t_y[0] + t_y[1] + t_z[0] + t_z[1]
-        diagonal = diagonal + WELL * fl[x].astype(jnp.float32)
+        t_y, t_z = (t_yz[x, 0], t_yz[x, 1]), (t_yz[x, 2], t_yz[x, 3])
+        diagonal = near_sum[x]
         negdiag[x] = -1.5 * diagonal
         scale = STEP / diagonal
         for b in range(2):
@@ -291,22 +277,16 @@
     def flow_yz(k, x, group):
         center = basis[k, :, x + 1, 8:16]
         total = -STEP * center.reshape(2, 2, 2, E, LANES)
+        halo = jnp.where(lax.rem(lane, 2) == 0, z_halo[k, group, 0], z_halo[k, group, 1])
+        ends = [pltpu.roll(halo, LANES - 2 * (n * 8 + x), 1) if n else
+                pltpu.roll(halo, lax.rem(LANES - 2 * x, LANES), 1) for n in range(8)]
         for side in range(2):
             near = basis[k, :, x + 1, 7 + 2 * side:15 + 2 * side].reshape(2, 2, 2, E, LANES)
             total = total + vy[:, side, x][None, :, None] * near
             edge = lane == (0, 127)[side]
-            halo = z_halo[k, group, side]
-            moved = []
-            for s in range(8):
-                place = s * 8 + x
-                shift = LANES - place if side == 0 else 127 - place
-                moved.append(
-                    jnp.where(
-                        edge,
-                        pltpu.roll(halo, shift, 1),
-                        pltpu.roll(center[s], (1, 127)[side], 1),
-                    )
-                )
+            moved = [
+                jnp.where(edge, ends[n], pltpu.roll(center[n], (1, 127)[side], 1)) for n in range(8)
+            ]
             near = jnp.stack(moved).reshape(2, 2, 2, E, LANES)
             total = total + vz[:, side, x][None, None] * near
         return total
@@ -322,10 +302,11 @@
     def pack_z(k, x, tiles):
         up, down = tiles
         for s in range(8):
-            place = s * 8 + x
+            place = 2 * (s * 8 + x)
+            before = lax.rem(place + 127, LANES)
             value = basis[k, s, x + 1, 8:16]
             up = jnp.where(lane == place, pltpu.roll(value, place + 1, 1), up)
-            down = jnp.where(lane == place, pltpu.roll(value, place, 1), down)
+            down = jnp.where(lane == before, pltpu.roll(value, before, 1), down)
         return up, down
 
     def copies(k):
@@ -357,24 +338,49 @@
     def inner_flow(k, x, group=0):
         return flow_yz(k, x, group) + flow_x(k, x, 0) + flow_x(k, x, 1)
 
-    arriving_x = []
-    for k in range(SWEEPS):
+    def pack_outer(k):
+        tiles = (zero, zero)
+        for x in (0, 7):
+            tiles = pack_z(k, x, tiles)
+        z_send[k, 1, 0], z_send[k, 1, 1] = tiles
+
+    arriving_x, arriving_inner, arriving_outer = copies(1)
+    for c in k_yz:
+        c.wait_recv()
+    for side in range(2):
+        for n, tile in enumerate(prepare(7 * side, (1 - side,))):
+            a_send[side, n] = tile
+    start(h_copies[2:4])
+
+    def first_inner(x, tiles):
+        total, t_y, t_z = prepare(x, (0, 1))
+        first_values(lambda n: mk[n, x], x + 1, par_x, STEP / total, None, t_y, t_z)
+        return pack_z(1, x, tiles)
+
+    tiles = lax.fori_loop(1, 7, first_inner, (zero, zero), unroll=True)
+    z_send[1, 0, 0], z_send[1, 0, 1] = tiles
+    start(arriving_inner)
+    for c in k_x:
+        c.wait_recv()
+    for side in range(2):
+        x = 7 * side
+        t_x = harmonic(kx[8 * side], kx[8 * side + 1])
+        near_sum[x] = a_send[side, 0] + t_x
+        first_values(
+            lambda n: mk[n, x], x + 1, par_x, STEP / near_sum[x], t_x, a_send[side, 1], a_send[side, 2]
+        )
+    pack_outer(1)
+    start(arriving_outer)
+
+    def weigh(x, carry):
+        weights(x)
+        return carry
+
+    lax.fori_loop(0, E, weigh, 0, unroll=True)
+    for k in range(1, SWEEPS):
         next_x, next_inner, next_outer = copies(k + 1)
-        if k == 0:
-            for c in k_yz:
-                c.wait_recv()
-            for side in range(2):
-                outer_plane(side)
-            start(h_copies[2:4])
-
-            def prepare(x, carry):
-                weights(x)
-                return carry
-
-            lax.fori_loop(1, 7, prepare, 0, unroll=True)
-        else:
-            for c in arriving_inner:
-                c.wait_recv()
+        for c in arriving_inner:
+            c.wait_recv()
 
         def inner(x, tiles):
             update(k, x, inner_flow(k, x))
@@ -383,14 +389,13 @@
         tiles = lax.fori_loop(1, 7, inner, (zero, zero), unroll=True)
         z_send[k + 1, 0, 0], z_send[k + 1, 0, 1] = tiles
         start(next_inner)
-        if k > 0:
-            for c in arriving_outer:
-                c.wait_recv()
-            for x, side in ((0, 1), (7, 0)):
-                part[k, 1 - side] = (flow_yz(k, x, 1) + flow_x(k, x, side)).reshape(8, E, LANES)
-            if k == 2:
-                start(h_copies[4:])
-        for c in (k_x, h_copies[:4], arriving_x, h_copies[4:])[k]:
+        for c in arriving_outer:
+            c.wait_recv()
+        for x, side in ((0, 1), (7, 0)):
+            part[k, 1 - side] = (flow_yz(k, x, 1) + flow_x(k, x, side)).reshape(8, E, LANES)
+        if k == 2:
+            start(h_copies[4:])
+        for c in (h_copies[:4], arriving_x, h_copies[4:])[k - 1]:
             c.wait_recv()
         for side in range(2):
             if k == 1:
@@ -398,18 +403,10 @@
             if k == 3:
                 third_halo(side)
         for x, side in ((0, 0), (7, 1)):
-            if k == 0:
-                weights(x)
-                flow = inner_flow(k, x, 1)
-            else:
-                flow = part[k, side].reshape(2, 2, 2, E, LANES) + flow_x(k, x, side)
-            update(k, x, flow)
+            update(k, x, part[k, side].reshape(2, 2, 2, E, LANES) + flow_x(k, x, side))
         if k % 2:
             start(next_x)
-        tiles = (zero, zero)
-        for x in (0, 7):
-            tiles = pack_z(k + 1, x, tiles)
-        z_send[k + 1, 1, 0], z_send[k + 1, 1, 1] = tiles
+        pack_outer(k + 1)
         start(next_outer)
         arriving_x, arriving_inner, arriving_outer = next_x, next_inner, next_outer
 
@@ -600,21 +597,30 @@
             if m_x == 0:
                 value = value + zf_halo[side, m_y + 1]
             packed = packed + jnp.where(takes, value, 0.0)
-        packed = packed + pltpu.roll(packed, 64, 1)
-        packed = packed + pltpu.roll(packed, 32, 1)
         target = 124 * side
         for h in range(2):
             for y in range(2):
-                shift = (target - (h * 2 + y)) % LANES
-                moved = pltpu.roll(packed, shift, 1) if shift else packed
-                whole[h][y] = whole[h][y] + jnp.where(lane == target, moved, 0.0)
+                total = None
+                for group in range(4):
+                    shift = (target - group * 32 - (h * 2 + y)) % LANES
+                    moved = pltpu.roll(packed, shift, 1) if shift else packed
+                    total = moved if total is None else total + moved
+                whole[h][y] = whole[h][y] + jnp.where(lane == target, total, 0.0)
     tiles = jnp.stack([whole[0][0], whole[0][1], whole[1][0], whole[1][1]])
-    lows, highs = tiles, pltpu.roll(tiles, 124, 2)
-    for b in range(4):
-        inside = lax.rem(lane, 2 ** (b + 4))
-        takes = (inside >= 2**b) & (inside < 2 ** (b + 1))
-        lows = jnp.where(takes, pltpu.roll(lows, LANES - 7 * 2**b, 2), lows)
-        highs = jnp.where(takes, pltpu.roll(highs, LANES - 7 * 2**b, 2), highs)
+
+    def gather(offset):
+        values = tiles
+        for step, (spread, size) in enumerate(((7, 1), (28, 4))):
+            result = None
+            for n in range(4):
+                shift = (LANES - spread * n - (0 if step else offset)) % LANES
+                moved = pltpu.roll(values, shift, 2) if shift else values
+                here = lax.rem(lane, 32) == n if step == 0 else lane // 4 == n
+                result = moved if result is None else jnp.where(here, moved, result)
+            values = result
+        return values
+
+    lows, highs = gather(0), gather(4)
     picks = {0: ((0,), 1), 1: ((0, 1), 0), 2: ((1,), 1)}
     for d_x in range(3):
         for d_y in range(3):
@@ -684,6 +690,8 @@
             vmem((2, 8, E, LANES), jnp.int32),
             vmem((2, 8, E, LANES), f32),
             vmem((2, E, LANES), f32),
+            vmem((E, 4, E, LANES), f32),
+            vmem((E, E, LANES), f32),
             dma((5,)),
             dma((6,)),
             dma((6,)),

time: 36.6 us -> 35.8 us (0.978)
  Pallas kernels: 34.5 us -> 33.7 us
    pallas_call x1, Pallas kernels: 34.5 us -> 33.7 us  [shards(): pl.pallas_call(kernel, out_shape=(pltpu.VMEM((8, E, E, LANES), f32), pltp...]
where the time goes in v4:
time: 35.8 us; the launch traced here: 35.7 us
  Pallas kernels  33.7 us (94%)
  local copies, waits for them, and re-layouts  1.32 us (4%)
  between operations  0.64 us (2%)
    pallas_call x1, Pallas kernels, shards(): pl.pallas_call(kernel, out_shape=(pltpu.VMEM((8, E, E, LANES), f32), pltp...  33.7 us

profile of v4, /device:TPU:25, one launch (start us, length us, event | category | flops | bytes accessed | tf_op | source)
XLA Modules:
  0.0 35.7 jit_solution(3395834987506331233)
XLA Ops:
  0.6 33.7 %smooth_and_contract.1 = (f32[8,8,8,128]{3,2,1,0:T(8,128)S(1)}, f32[27,16]{1,0:T(8,128)S(1)}) custom-call(f32[3,8,8,128]{3,2,1,0:T(8,128)} %perm.1, s32[8,8,128]{2,1,0:T(8,128)} %flags.1, s32[8,8,8,128]{3,2,1,0:T(8,128)} %mask.1), custom_call_target="tpu_custom_call" | custom-call | tf_op jit(solution)/shard_map/smooth_and_contract/pallas_call | solution.py:649
  34.4 0.7 %copy.8 = f32[8,8,8,128]{3,2,1,0:T(8,128)} copy(f32[8,8,8,128]{3,2,1,0:T(8,128)S(1)} %get-tuple-element.10) | data formatting | bytes 524288
  35.1 0.6 %reshape.8 = f32[3,3,3,1,1,16]{5,4,3,2,1,0:T(1,128)} reshape(f32[27,16]{1,0:T(8,128)S(1)} %get-tuple-element.5) | data formatting | bytes 3456 | tf_op jit(solution)/shard_map/reshape | solution.py:711

commit v5 on v4

--- a/solution.py
+++ b/solution.py
@@ -1,3 +1,5 @@
+import functools
+
 import jax
 import jax.numpy as jnp
 from jax import lax
@@ -25,6 +27,7 @@
     kx, ky, kz, kz_send, kz_halo, fl, mk, basis, z_send, z_halo,
     vx, vy, vz, negdiag, part, pz, iz, sums, rows, rows_x, rows_y, rows_d, zr_send, zr_halo,
     faces, face_sums, face_rows, face_rows_y, zf_send, zf_halo, a_send, a_halo, mask_halo, part_halo, halo_vx, t_yz, near_sum,
+    y_faces, y_sums, z_near, z_near_w, z_own_w, z_sums, rows2, rows2_x, rows2_y, rows2_d, zg_send, zg_halo,
     load_sem, k_send, k_recv, p_send, p_recv, r_send, r_recv, h_send, h_recv, out_sem,
 ):
     at = {axis: lax.axis_index(axis) for axis in AXES}
@@ -102,10 +105,12 @@
             kx[k_plane] = zero
             a_halo[side] = jnp.ones((3, E, LANES), jnp.float32)
             mask_halo[side] = jnp.zeros((8, E, LANES), jnp.int32)
-            part_halo[side] = jnp.zeros((8, E, LANES), jnp.float32)
+            for n in range(2):
+                part_halo[n, side] = jnp.zeros((8, E, LANES), jnp.float32)
             for k in range(1, SWEEPS + 1):
                 basis[k, :, k_plane, 8:16] = jnp.zeros((8, E, LANES), jnp.float32)
             rows_x[side] = jnp.zeros((2, E, LANES), jnp.float32)
+            rows2_x[side] = jnp.zeros((2, E, LANES), jnp.float32)
 
         @pl.when(jnp.logical_not(has["gy", d]))
         def _():
@@ -113,13 +118,14 @@
             ky[:, y_row:y_row + 1] = jnp.zeros((E, 1, LANES), jnp.float32)
 
             def clear(i, carry):
-                basis[1 + i // 8, lax.rem(i, 8), 1:9, y_row:y_row + 1] = jnp.zeros(
+                basis[i // 8, lax.rem(i, 8), 1:9, y_row:y_row + 1] = jnp.zeros(
                     (E, 1, LANES), jnp.float32
                 )
                 return carry
 
             lax.fori_loop(0, 8 * SWEEPS, clear, 0)
             rows_y[side] = jnp.zeros((2, E, LANES), jnp.float32)
+            rows2_y[side] = jnp.zeros((2, E, LANES), jnp.float32)
             face_rows_y[side] = jnp.zeros((2, E, LANES), jnp.float32)
 
         @pl.when(jnp.logical_not(has["gz", d]))
@@ -133,6 +139,7 @@
             @pl.when(jnp.logical_not(has["gx", d] & has["gy", e]))
             def _():
                 rows_d[side, (e + 1) // 2] = zero
+                rows2_d[side, (e + 1) // 2] = zero
 
     for m_z in (1, -1):
         side = (1 - m_z) // 2
@@ -151,6 +158,22 @@
                 @pl.when(jnp.logical_not(there))
                 def _():
                     zr_halo[side, m_x + 1, m_y + 1] = zero
+
+        for m_x in (1, 0, -1):
+            there = has["gz", -m_z]
+            if m_x:
+                there = there & has["gx", -m_x]
+
+            @pl.when(jnp.logical_not(there))
+            def _():
+                zg_halo[side, m_x + 1] = zero
+
+    def close(i, carry):
+        basis[SWEEPS, i, 1:9, 7:8] = jnp.zeros((E, 1, LANES), jnp.float32)
+        basis[SWEEPS, i, 1:9, 16:17] = jnp.zeros((E, 1, LANES), jnp.float32)
+        return carry
+
+    lax.fori_loop(0, 8, close, 0)
 
     for load in loads[:3]:
         load.wait()
@@ -177,14 +200,15 @@
     for load in loads[3:]:
         load.wait()
     h_copies = []
-    for src, dst in ((mk, mask_halo), (a_send, a_halo), (part, part_halo)):
+    for src, dst in (
+        (lambda side: mk.at[:, 7 * side], mask_halo),
+        (lambda side: a_send.at[side], a_halo),
+        (lambda side: part.at[2, side], part_halo.at[0]),
+        (lambda side: part.at[3, side], part_halo.at[1]),
+    ):
         for side, d in ((0, -1), (1, 1)):
             n = len(h_copies)
-            if src is mk:
-                block = mk.at[:, 7 * side]
-            else:
-                block = src.at[2, side] if src is part else src.at[side]
-            h_copies.append(Copy(block, dst.at[1 - side], h_send.at[n], h_recv.at[n], (("gx", d),)))
+            h_copies.append(Copy(src(side), dst.at[1 - side], h_send.at[n], h_recv.at[n], (("gx", d),)))
     start(h_copies[:2])
 
     def faces_yz(x):
@@ -242,12 +266,12 @@
             lambda n: mask_halo[side, n], 9 * side, 1 - par_x, scale, t_x, a_halo[side, 1], a_halo[side, 2]
         )
 
-    def third_halo(side):
+    def next_halo(k, side):
         plane = 9 * side
-        flow = part_halo[side] + halo_vx[side] * basis[2, :, 1 + 7 * side, 8:16]
-        center = basis[2, :, plane, 8:16]
+        flow = part_halo[k - 2, side] + halo_vx[side] * basis[k, :, 1 + 7 * side, 8:16]
+        center = basis[k, :, plane, 8:16]
         change = mask_halo[side].astype(jnp.float32) * flow
-        basis[3, :, plane, 8:16] = center + change - center * jnp.sum(change, axis=0)
+        basis[k + 1, :, plane, 8:16] = center + change - center * jnp.sum(change, axis=0)
 
     def weights(x):
         here = kx[x + 1]
@@ -274,12 +298,15 @@
         near = basis[k, :, x + 2 * side, 8:16].reshape(2, 2, 2, E, LANES)
         return vx[:, side, x][:, None, None] * near
 
-    def flow_yz(k, x, group):
+    def z_ends(k, x, group):
+        halo = jnp.where(lax.rem(lane, 2) == 0, z_halo[k, group, 0], z_halo[k, group, 1])
+        first = pltpu.roll(halo, lax.rem(LANES - 2 * x, LANES), 1)
+        return [first] + [pltpu.roll(halo, LANES - 2 * (n * 8 + x), 1) for n in range(1, 8)]
+
+    def flow_yz(k, x, group, closed=False):
         center = basis[k, :, x + 1, 8:16]
         total = -STEP * center.reshape(2, 2, 2, E, LANES)
-        halo = jnp.where(lax.rem(lane, 2) == 0, z_halo[k, group, 0], z_halo[k, group, 1])
-        ends = [pltpu.roll(halo, LANES - 2 * (n * 8 + x), 1) if n else
-                pltpu.roll(halo, lax.rem(LANES - 2 * x, LANES), 1) for n in range(8)]
+        ends = [zero] * 8 if closed else z_ends(k, x, group)
         for side in range(2):
             near = basis[k, :, x + 1, 7 + 2 * side:15 + 2 * side].reshape(2, 2, 2, E, LANES)
             total = total + vy[:, side, x][None, :, None] * near
@@ -311,12 +338,13 @@
 
     def copies(k):
         ref = basis.at[k]
+        y_target = basis.at[k % SWEEPS]
         own = pl.ds(8, E)
         sems = [(p_send.at[k, i], p_recv.at[k, i]) for i in range(12)]
         x = [
             Copy(ref.at[:, 8, own], ref.at[:, 0, own], *sems[0], (("gx", 1),)),
             Copy(ref.at[:, 1, own], ref.at[:, 9, own], *sems[1], (("gx", -1),)),
-        ] if k % 2 == 0 else []
+        ] if k == 2 else []
         yz = []
         for group in range(2):
             part_yz = []
@@ -324,7 +352,7 @@
                 at_sem = 2 + 2 * group + 2 * n
                 for side, (a, b, d) in enumerate(((15, 7, 1), (8, 16, -1))):
                     part_yz.append(Copy(
-                        ref.at[:, planes, pl.ds(a, 1)], ref.at[:, planes, pl.ds(b, 1)],
+                        ref.at[:, planes, pl.ds(a, 1)], y_target.at[:, planes, pl.ds(b, 1)],
                         *sems[at_sem + side], (("gy", d),),
                     ))
             for side, d in ((0, 1), (1, -1)):
@@ -393,18 +421,18 @@
             c.wait_recv()
         for x, side in ((0, 1), (7, 0)):
             part[k, 1 - side] = (flow_yz(k, x, 1) + flow_x(k, x, side)).reshape(8, E, LANES)
-        if k == 2:
-            start(h_copies[4:])
-        for c in (h_copies[:4], arriving_x, h_copies[4:])[k - 1]:
+        if k >= 2:
+            start(h_copies[2 * k:2 * k + 2])
+        for c in (h_copies[:4], arriving_x, h_copies[4:6])[k - 1]:
             c.wait_recv()
         for side in range(2):
             if k == 1:
                 first_halo(side)
             if k == 3:
-                third_halo(side)
+                next_halo(2, side)
         for x, side in ((0, 0), (7, 1)):
             update(k, x, part[k, side].reshape(2, 2, 2, E, LANES) + flow_x(k, x, side))
-        if k % 2:
+        if k == 1:
             start(next_x)
         pack_outer(k + 1)
         start(next_outer)
@@ -429,21 +457,18 @@
         return carry
 
     lax.fori_loop(0, E, split_basis, 0, unroll=True)
-    for c in arriving_inner + arriving_outer:
-        c.wait_recv()
-
     def image(x, flow):
         own, beside = split_z(flow * negdiag[x])
         iz[:, 0, x] = own
         iz[:, 1, x] = beside
 
-    def inner_image(x, carry):
-        image(x, inner_flow(SWEEPS, x))
+    def closed_image(x, carry):
+        image(x, flow_yz(SWEEPS, x, 0, True) + flow_x(SWEEPS, x, 0) + flow_x(SWEEPS, x, 1))
         return carry
 
-    lax.fori_loop(1, 7, inner_image, 0, unroll=True)
+    lax.fori_loop(1, 7, closed_image, 0, unroll=True)
     for x, side in ((0, 1), (7, 0)):
-        image(x, flow_yz(SWEEPS, x, 1) + flow_x(SWEEPS, x, side))
+        image(x, flow_yz(SWEEPS, x, 0, True) + flow_x(SWEEPS, x, side))
 
     def pair_of(a_x, a_y):
         return lax.rem(a_x + par_x, 2) * 2 + lax.rem(a_y + par_y, 2)
@@ -463,13 +488,18 @@
 
     lax.fori_loop(0, 8, contract, 0, unroll=2)
 
-    def halves(ref, count):
+    def y_halves(ref, count):
         results = []
         for y_half in range(2):
             total = ref[pl.ds(4 * y_half, count * 8, stride=8)]
             for y in range(1, 4):
                 total = total + ref[pl.ds(4 * y_half + y, count * 8, stride=8)]
-            total = total.reshape(count, E, LANES)
+            results.append(total.reshape(count, E, LANES))
+        return results
+
+    def halves(ref, count):
+        results = []
+        for total in y_halves(ref, count):
             total = total + pltpu.roll(total, 127, 2)
             total = total + pltpu.roll(total, 126, 2)
             results.append(total.reshape(count // 2, 2, E, LANES))
@@ -529,9 +559,103 @@
     start(row_copies[first:])
     first = len(row_copies)
 
-    for c in arriving_x:
+    flat = basis.reshape((SWEEPS + 1) * 8 * 240, LANES)
+    flat_t = t_yz.reshape(E * 4 * E, LANES)
+    def z_faces(planes):
+        for x in planes:
+            ends = jnp.stack(z_ends(SWEEPS, x, 1 if x in (0, 7) else 0))
+            for n, tiles in enumerate(split_z(ends)):
+                z_near[:, n, x] = tiles
+                z_near_w[:, n, x] = tiles * z_weight(x)
+
+    def z_weight(x):
+        return -jnp.where(lane == 0, t_yz[x, 2], jnp.where(lane == 127, t_yz[x, 3], 0.0))
+
+    def contract_z(first_planes, i, carry):
+        half, a_x, a_y = i // 4, lax.rem(i // 2, 2), lax.rem(i, 2)
+        s_xy = pair_of(a_x, a_y)
+        planes = [1 + 3 * half + j for j in range(3)] if first_planes else [7 * half]
+        for e in range(8):
+            u_xy = pair_of(a_x + e // 4, a_y + e // 2 % 2)
+            place = pl.ds(pl.multiple_of(i * 64, 64) + e * 8, E)
+            total = None if first_planes else z_sums[place]
+            for x in planes:
+                term = pz[s_xy, 0, x] * z_near_w[u_xy, e % 2, x] + z_near[s_xy, 0, x] * z_own_w[u_xy, e % 2, x]
+                total = term if total is None else total + term
+            z_sums[place] = total
+        return carry
+
+    for x in range(E):
+        for n in range(2):
+            z_own_w[:, n, x] = pz[:, n, x] * z_weight(x)
+    for c in arriving_inner:
+        c.wait_recv()
+    z_faces(range(1, 7))
+    lax.fori_loop(0, 8, functools.partial(contract_z, True), 0, unroll=2)
+    for c in arriving_outer:
         c.wait_recv()
     for side in range(2):
+        weight = -flat_t[pl.ds(side * 15, E, stride=32)]
+        for n, (k, y_row) in enumerate(((SWEEPS, 8 + 7 * side), (0, 7 + 9 * side))):
+            tiles = jnp.stack([flat[pl.ds((k * 8 + m) * 240 + 24 + y_row, E, stride=24)] for m in range(8)])
+            own, beside = split_z(tiles)
+            y_faces[side, n, 0, :, 0] = own
+            y_faces[side, n, 0, :, 1] = beside
+            y_faces[side, n, 1, :, 0] = own * weight
+            y_faces[side, n, 1, :, 1] = beside * weight
+
+    def contract_y(i, carry):
+        side, a_x = i // 2, lax.rem(i, 2)
+        s_xy = pair_of(a_x, 0)
+        for a_z in range(2):
+            for e in range(8):
+                u_xy = pair_of(a_x + e // 4, e // 2 % 2)
+                u_z = (a_z + e) % 2
+                total = y_faces[side, 0, 0, s_xy, a_z] * y_faces[side, 1, 1, u_xy, u_z]
+                total = total + y_faces[side, 1, 0, s_xy, a_z] * y_faces[side, 0, 1, u_xy, u_z]
+                y_sums[pl.ds(pl.multiple_of((i * 2 + a_z) * 64, 64) + e * 8, E)] = total
+        return carry
+
+    lax.fori_loop(0, 4, contract_y, 0, unroll=True)
+    y_quarter = halves(y_sums, 8)
+    entries = []
+    for i in range(4):
+        side, a_x = i // 2, i % 2
+        for x_half in range(2):
+            entries.append((a_x * 64 + (x_half ^ a_x) * 2 + side, y_quarter[x_half][i, 1]))
+    zg_send[0], zg_send[1] = pack_rows(entries)
+    for side, m_z in ((0, 1), (1, -1)):
+        for m_x in (1, -1, 0):
+            move_rows(zg_send.at[side], zg_halo.at[side, m_x + 1], (("gx", m_x), ("gz", m_z)))
+    start(row_copies[first:])
+    first = len(row_copies)
+
+    z_faces((0, 7))
+    lax.fori_loop(0, 8, functools.partial(contract_z, False), 0, unroll=2)
+    z_quarter = y_halves(z_sums, 8)
+    y_merged = [merge_z(part_of) for part_of in y_quarter]
+    for y_half in range(2):
+        tiles = jnp.where(lane == 0, z_quarter[y_half], 0.0)
+        tiles = tiles + jnp.where(lane == 124, pltpu.roll(z_quarter[y_half], 125, 2), 0.0)
+        for i in range(8):
+            half, a_x, a_y = i // 4, i // 2 % 2, i % 2
+            tile = tiles[i] if a_y else tiles[i] + y_merged[half][y_half * 2 + a_x]
+            rows2[a_x, a_y, half, y_half] = tile
+    for side, d in ((0, 1), (1, -1)):
+        for side_y, d_y in ((0, 1), (1, -1)):
+            move_rows(
+                rows2.at[1, 1, 1 - side, 1 - side_y], rows2_d.at[side, side_y], (("gx", d), ("gy", d_y))
+            )
+    for side, d in ((0, 1), (1, -1)):
+        move_rows(rows2.at[1, 0, 1 - side], rows2_x.at[side], (("gx", d),))
+        move_rows(rows2.at[0, 1, :, 1 - side], rows2_y.at[side], (("gy", d),))
+    start(row_copies[first:])
+    first = len(row_copies)
+
+    for c in h_copies[6:]:
+        c.wait_recv()
+    for side in range(2):
+        next_halo(3, side)
         x = 7 * side
         weight = vx[0, side, x] * negdiag[x]
         for n, plane in enumerate((x + 1, 9 * side)):
@@ -580,6 +704,7 @@
     whole = [
         [
             rows[0, 0, h, y] + rows_x[h, y] + rows_y[y, h] + rows_d[h, y] + face_own[y][h] + face_rows_y[y, h]
+            + (rows2[0, 0, h, y] + rows2_x[h, y] + rows2_y[y, h] + rows2_d[h, y])
             for y in range(2)
         ]
         for h in range(2)
@@ -596,6 +721,8 @@
             value = zr_halo[side, m_x + 1, m_y + 1]
             if m_x == 0:
                 value = value + zf_halo[side, m_y + 1]
+            if m_y == 0:
+                value = value + zg_halo[side, m_x + 1]
             packed = packed + jnp.where(takes, value, 0.0)
         target = 124 * side
         for h in range(2):
@@ -688,19 +815,31 @@
             vmem((2, 3, E, LANES), f32),
             vmem((2, 3, E, LANES), f32),
             vmem((2, 8, E, LANES), jnp.int32),
-            vmem((2, 8, E, LANES), f32),
+            vmem((2, 2, 8, E, LANES), f32),
             vmem((2, E, LANES), f32),
             vmem((E, 4, E, LANES), f32),
             vmem((E, E, LANES), f32),
+            vmem((2, 2, 2, 4, 2, E, LANES), f32),
+            vmem((512, LANES), f32),
+            vmem((4, 2, E, E, LANES), f32),
+            vmem((4, 2, E, E, LANES), f32),
+            vmem((4, 2, E, E, LANES), f32),
+            vmem((512, LANES), f32),
+            vmem((2, 2, 2, 2, E, LANES), f32),
+            vmem((2, 2, E, LANES), f32),
+            vmem((2, 2, E, LANES), f32),
+            vmem((2, 2, E, LANES), f32),
+            vmem((2, E, LANES), f32),
+            vmem((2, 3, E, LANES), f32),
             dma((5,)),
             dma((6,)),
             dma((6,)),
             dma((SWEEPS + 1, 12)),
             dma((SWEEPS + 1, 12)),
-            dma((34,)),
-            dma((34,)),
-            dma((6,)),
-            dma((6,)),
+            dma((48,)),
+            dma((48,)),
+            dma((8,)),
+            dma((8,)),
             dma((1,)),
         ],
         compiler_params=pltpu.CompilerParams(

time: 35.8 us -> 35.3 us (0.986)
  Pallas kernels: 33.7 us -> 33.2 us
    pallas_call x1, Pallas kernels: 33.7 us -> 33.2 us  [shards(): pl.pallas_call(kernel, out_shape=(pltpu.VMEM((8, E, E, LANES), f32), pltp...]
where the time goes in v5:
time: 35.3 us; the launch traced here: 35.2 us
  Pallas kernels  33.2 us (94%)
  local copies, waits for them, and re-layouts  1.32 us (4%)
  between operations  0.64 us (2%)
    pallas_call x1, Pallas kernels, shards(): pl.pallas_call(kernel, out_shape=(pltpu.VMEM((8, E, E, LANES), f32), pltp...  33.2 us

profile of v5, /device:TPU:25, one launch (start us, length us, event | category | flops | bytes accessed | tf_op | source)
XLA Modules:
  0.0 35.2 jit_solution(3630964774571725232)
XLA Ops:
  0.6 33.2 %smooth_and_contract.1 = (f32[8,8,8,128]{3,2,1,0:T(8,128)S(1)}, f32[27,16]{1,0:T(8,128)S(1)}) custom-call(f32[3,8,8,128]{3,2,1,0:T(8,128)} %perm.1, s32[8,8,128]{2,1,0:T(8,128)} %flags.1, s32[8,8,8,128]{3,2,1,0:T(8,128)} %mask.1), custom_call_target="tpu_custom_call" | custom-call | tf_op jit(solution)/shard_map/smooth_and_contract/pallas_call | solution.py:776
  33.8 0.7 %copy.8 = f32[8,8,8,128]{3,2,1,0:T(8,128)} copy(f32[8,8,8,128]{3,2,1,0:T(8,128)S(1)} %get-tuple-element.10) | data formatting | bytes 524288
  34.5 0.6 %reshape.8 = f32[3,3,3,1,1,16]{5,4,3,2,1,0:T(1,128)} reshape(f32[27,16]{1,0:T(8,128)S(1)} %get-tuple-element.5) | data formatting | bytes 3456 | tf_op jit(solution)/shard_map/reshape | solution.py:850

commit v6 on v5

--- a/solution.py
+++ b/solution.py
@@ -432,10 +432,10 @@
                 next_halo(2, side)
         for x, side in ((0, 0), (7, 1)):
             update(k, x, part[k, side].reshape(2, 2, 2, E, LANES) + flow_x(k, x, side))
+        pack_outer(k + 1)
+        start(next_outer)
         if k == 1:
             start(next_x)
-        pack_outer(k + 1)
-        start(next_outer)
         arriving_x, arriving_inner, arriving_outer = next_x, next_inner, next_outer
 
     out = pltpu.make_async_copy(
@@ -759,13 +759,23 @@
                     low_tile = lows[n] if low_tile is None else low_tile + lows[n]
                     high_tile = highs[n] if high_tile is None else high_tile + highs[n]
             e = e_x * 4 + e_y * 2
-            out_row = (d_x * 3 + d_y) * 3
-            out_c[out_row:out_row + 1, :] = low_tile[e + 1:e + 2, :16]
-            out_c[out_row + 1:out_row + 2, :] = low_tile[e:e + 1, :16] + high_tile[e:e + 1, :16]
-            out_c[out_row + 2:out_row + 3, :] = high_tile[e + 1:e + 2, :16]
+            out_c[d_x, d_y, 0, 0, 0:1] = low_tile[e + 1:e + 2, :16]
+            out_c[d_x, d_y, 1, 0, 0:1] = low_tile[e:e + 1, :16] + high_tile[e:e + 1, :16]
+            out_c[d_x, d_y, 2, 0, 0:1] = high_tile[e + 1:e + 2, :16]
     out.wait()
     for c in started:
         c.wait_send()
+
+
+def hand_over(p_ref, c_ref, out_p, out_c, sem):
+    copies = [
+        pltpu.make_async_copy(p_ref, out_p, sem.at[0]),
+        pltpu.make_async_copy(c_ref, out_c, sem.at[1]),
+    ]
+    for copy in copies:
+        copy.start()
+    for copy in copies:
+        copy.wait()
 
 
 def shards(permeability, well_flags, support_mask):
@@ -777,7 +787,7 @@
         kernel,
         out_shape=(
             pltpu.VMEM((8, E, E, LANES), f32),
-            pltpu.VMEM((27, 16), f32),
+            pltpu.VMEM((3, 3, 3, 1, 1, 16), f32),
         ),
         in_specs=[any_spec] * 3,
         out_specs=(pl.BlockSpec(memory_space=pltpu.VMEM), pl.BlockSpec(memory_space=pltpu.VMEM)),
@@ -847,7 +857,19 @@
         ),
         name="smooth_and_contract",
     )(permeability, well_flags, support_mask)
-    return prolongation, coarse.reshape(3, 3, 3, 1, 1, 16)
+    hbm_spec = pl.BlockSpec(memory_space=pltpu.HBM)
+    return pl.pallas_call(
+        hand_over,
+        out_shape=(
+            jax.ShapeDtypeStruct((8, E, E, LANES), f32),
+            jax.ShapeDtypeStruct((3, 3, 3, 1, 1, 16), f32),
+        ),
+        in_specs=[pl.BlockSpec(memory_space=pl.ANY)] * 2,
+        out_specs=(hbm_spec, hbm_spec),
+        scratch_shapes=[dma((2,))],
+        compiler_params=pltpu.CompilerParams(vmem_limit_bytes=4 * 1024 * 1024),
+        name="hand_over",
+    )(prolongation, coarse)
 
 
 def solution(mesh):

time: 35.3 us -> 34.9 us (0.989)
  local copies, waits for them, and re-layouts: 1.32 us -> 0 us
  Pallas kernels: 33.2 us -> 34.1 us
    pallas_call x0 -> x1, Pallas kernels: none -> 0.72 us  [shards(): pl.pallas_call(hand_over, out_shape=(jax.ShapeDtypeStruct((8, E, E, LANES...]
    unnamed x1 -> x0, local copies, waits for them, and re-layouts: 0.71 us -> none
    reshape x1 -> x0, local copies, waits for them, and re-layouts: 0.62 us -> none  [shards(): return (prolongation, coarse.reshape(3, 3, 3, 1, 1, 16))]
where the time goes in v6:
time: 34.9 us; the launch traced here: 34.7 us
  Pallas kernels  34.1 us (98%)
  between operations  0.64 us (2%)
    pallas_call x1, Pallas kernels, shards(): pl.pallas_call(kernel, out_shape=(pltpu.VMEM((8, E, E, LANES), f32), pltp...  33.4 us
    pallas_call x1, Pallas kernels, shards(): pl.pallas_call(hand_over, out_shape=(jax.ShapeDtypeStruct((8, E, E, LANES...  0.72 us

profile of v6, /device:TPU:25, one launch (start us, length us, event | category | flops | bytes accessed | tf_op | source)
XLA Modules:
  0.0 34.7 jit_solution(9990785645770315879)
XLA Ops:
  0.6 33.4 %smooth_and_contract.1 = (f32[8,8,8,128]{3,2,1,0:T(8,128)S(1)}, f32[3,3,3,1,1,16]{5,4,3,2,1,0:T(1,128)S(1)}) custom-call(f32[3,8,8,128]{3,2,1,0:T(8,128)} %perm.1, s32[8,8,128]{2,1,0:T(8,128)} %flags.1, s32[8,8,8,128]{3,2,1,0:T(8,128)} %mask.1), custom_call_target="tpu_custom_call" | custom-call | tf_op jit(solution)/shard_map/smooth_and_contract/pallas_call | solution.py:786
  34.0 0.7 %hand_over.1 = (f32[8,8,8,128]{3,2,1,0:T(8,128)}, f32[3,3,3,1,1,16]{5,4,3,2,1,0:T(1,128)}) custom-call(f32[8,8,8,128]{3,2,1,0:T(8,128)S(1)} %get-tuple-element.4.p_ref, f32[3,3,3,1,1,16]{5,4,3,2,1,0:T(1,128)S(1)} %get-tuple-element.5.c_ref), custom_call_target="tpu_custom_call" | custom-call | tf_op jit(solution)/shard_map/hand_over/pallas_call | solution.py:861
